TPU v7x, 128 devices: a whole 4x4x4 slice. The times are simulated.
128 devices in a mesh: dp: 8 (over y, z_lo), ctx: 16 (over x, z_hi, core).
Axes of the slice: x: 4, y: 4, z: 4 (z_hi: 2, z_lo: 2; z = z_hi * 2 + z_lo), core: 2. Of those that a mesh axis runs over, the one named last changes fastest.
Arguments:
- uvqk: bfloat16 [8, 2048, 4096], P('dp', 'ctx'), may hold values from -6 to 6
- residual: bfloat16 [8, 2048, 1024], P('dp', 'ctx'), may hold values from -6 to 6
- lengths: int32 [8, 8], P('dp'), may hold values from 1 to 1024, 2048 in all within a row
- time_buckets: int32 [8, 2048], P('dp', 'ctx'), may hold values from 0 to 15
- pos_table: float32 [8, 16], replicated, may hold values from -4 to 4
- time_table: float32 [8, 16], replicated, may hold values from -4 to 4
- output_norm_gain: float32 [1024], replicated, may hold values from 0.5 to 1.5
- w_out: bfloat16 [1024, 1024], replicated, may hold values from -0.1875 to 0.1875
- cotangent: bfloat16 [8, 2048, 1024], P('dp', 'ctx'), may hold values from -6 to 6
Outputs:
- layer_out: bfloat16 [8, 2048, 1024], P('dp', 'ctx')
- d_uvqk: bfloat16 [8, 2048, 4096], P('dp', 'ctx')
- d_w_out: float32 [1024, 1024], P(('dp', 'ctx'))
- d_norm_gain: float32 [1024], replicated
- d_pos_table: float32 [8, 16], replicated
- d_time_table: float32 [8, 16], replicated
Inputs may be any that keep to these rules, and one draw needn't show every extreme that they name: `lengths`: each row sums to 2048, and its largest entry is exactly 1024.
All inputs are finite; a program needn't handle non-finite values.
Results may differ from a plain program's by a relative error of at most 0.0066.
Values may be sent and summed in bfloat16 or wider, within the bound.
A program may use at most 128 MiB of HBM per device.

v0:
```python
import jax
import jax.numpy as jnp
from jax import lax
from jax.sharding import PartitionSpec as P

HEADS = 8


EPS = 1e-05


def shifted(value, axis, steps):
    count = lax.axis_size(axis)
    first, last = (max(0, -steps), min(count, count - steps))
    return lax.ppermute(value, axis, [(source, source + steps) for source in range(first, last)])


def silu_grad(value):
    sig = jax.nn.sigmoid(value)
    return sig * (1.0 + value * (1.0 - sig))


def pair_masks(query_pos, key_pos, query_user, key_user, query_time, key_time, buckets, maxlen):
    gap = query_pos[:, None] - key_pos[None, :]
    allowed = jnp.logical_and(query_user[:, None] == key_user[None, :], gap >= 0)
    pos_bucket = jnp.minimum(jnp.maximum(gap, 0) * buckets // maxlen, buckets - 1)
    time_gap = jnp.abs(query_time[:, None] - key_time[None, :])
    return (allowed, pos_bucket, time_gap)


def bias_of(pos_table, time_table, pos_bucket, time_gap):
    total = jnp.zeros((pos_table.shape[0],) + pos_bucket.shape, jnp.float32)
    for bucket in range(pos_table.shape[1]):
        total = total + jnp.where(
            pos_bucket[None] == bucket, pos_table[:, bucket][:, None, None], 0.0
        )
    for bucket in range(time_table.shape[1]):
        total = total + jnp.where(
            time_gap[None] == bucket, time_table[:, bucket][:, None, None], 0.0
        )
    return total


def table_grad(d_scores, pos_bucket, time_gap, pos_count, time_count):
    columns = [
        jnp.sum(jnp.where(pos_bucket[None] == bucket, d_scores, 0.0), axis=(1, 2))
        for bucket in range(pos_count)
    ]
    columns = columns + [
        jnp.sum(jnp.where(time_gap[None] == bucket, d_scores, 0.0), axis=(1, 2))
        for bucket in range(time_count)
    ]
    return jnp.stack(columns, axis=1)


def body(
    uvqk, residual, lengths, time_buckets, pos_table, time_table, output_norm_gain, w_out, cotangent
):
    pre = uvqk[0]
    rows = pre.shape[0]
    width = residual.shape[2]
    hsize = width // HEADS
    scale = hsize ** (-0.5)
    count = lax.axis_size("ctx")
    myself = lax.axis_index("ctx")
    maxlen = count * rows // 2
    pos_count = pos_table.shape[1]
    time_count = time_table.shape[1]
    act = jax.nn.silu(pre.astype(jnp.float32)).astype(jnp.bfloat16)
    u_act = act[:, :width]
    keys_values = jnp.concatenate([act[:, 3 * width :], act[:, width : 2 * width]], axis=1)
    query_heads = act[:, 2 * width : 3 * width].reshape(rows, HEADS, hsize)
    ends = jnp.cumsum(lengths[0])
    local_rows = jnp.arange(rows, dtype=jnp.int32)
    own_time = time_buckets[0]

    def user_of(where):
        return jnp.sum((where[:, None] >= ends[None, :]).astype(jnp.int32), axis=1)

    def place(source):
        where = source * rows + local_rows
        return (where, user_of(where))

    last_step = count - 1

    def split_heads(block):
        return block.reshape(rows, HEADS, hsize)

    own_pos, own_user = place(myself)

    def attend(kv_block, key_time, key_src):
        key_pos, key_user = place(key_src)
        allowed, pos_bucket, time_gap = pair_masks(
            own_pos, key_pos, own_user, key_user, own_time, key_time, pos_count, maxlen
        )
        bias = bias_of(pos_table, time_table, pos_bucket, time_gap)
        scores = (
            jnp.einsum(
                "qhe,khe->hqk",
                query_heads,
                split_heads(kv_block[:, :width]),
                preferred_element_type=jnp.float32,
            )
            * scale
            + bias
        )
        weights = jnp.where(allowed[None], jax.nn.silu(scores), 0.0).astype(jnp.bfloat16)
        return jnp.einsum(
            "hqk,khe->qhe",
            weights,
            split_heads(kv_block[:, width:]),
            preferred_element_type=jnp.float32,
        ).reshape(rows, width)

    steps = jnp.arange(1, last_step + 1, dtype=jnp.int32)

    def forward_step(carry, step):
        total, kv_block, key_time = carry
        kv_block, key_time = shifted((kv_block, key_time), "ctx", 1)
        key_src = (myself - step) % count
        total = total + attend(kv_block, key_time, key_src)
        return ((total, kv_block, key_time), (kv_block, key_time))

    first_out = attend(keys_values, own_time, myself)
    (attended, _, _), kept = lax.scan(forward_step, (first_out, keys_values, own_time), steps)
    row_average = jnp.mean(attended, axis=1, keepdims=True)
    mean_removed = attended - row_average
    var = jnp.mean(mean_removed * mean_removed, axis=1, keepdims=True)
    inverse_deviation = lax.rsqrt(var + EPS)
    standardized_input = mean_removed * inverse_deviation
    normalized_rows = standardized_input * output_norm_gain[None, :]
    u_float = u_act.astype(jnp.float32)
    hidden = (normalized_rows * u_float).astype(jnp.bfloat16)
    cot = cotangent[0]
    output = (
        residual[0].astype(jnp.float32) + jnp.dot(hidden, w_out, preferred_element_type=jnp.float32)
    ).astype(jnp.bfloat16)
    d_hidden = lax.dot_general(
        cot, w_out, (((1,), (1,)), ((), ())), preferred_element_type=jnp.float32
    )
    d_u = d_hidden * normalized_rows
    normalized_gradient = d_hidden * u_float
    gain_product = jnp.sum(normalized_gradient * standardized_input, axis=0)
    gain_scaled = normalized_gradient * output_norm_gain[None, :]
    attended_gradient = (
        inverse_deviation
        * (
            gain_scaled
            - jnp.mean(gain_scaled, axis=1, keepdims=True)
            - standardized_input * jnp.mean(gain_scaled * standardized_input, axis=1, keepdims=True)
        )
    ).astype(jnp.bfloat16)
    query_grad = jnp.concatenate([act[:, 2 * width : 3 * width], attended_gradient], axis=1)

    def grad_pair(
        qdo_block, query_time, query_src, kv_block, key_time, key_src, want_query, want_keys
    ):
        query_pos, query_user = place(query_src)
        key_pos, key_user = place(key_src)
        allowed, pos_bucket, time_gap = pair_masks(
            query_pos, key_pos, query_user, key_user, query_time, key_time, pos_count, maxlen
        )
        bias = bias_of(pos_table, time_table, pos_bucket, time_gap)
        q_part = split_heads(qdo_block[:, :width])
        d_part = split_heads(qdo_block[:, width:])
        k_part = split_heads(kv_block[:, :width])
        v_part = split_heads(kv_block[:, width:])
        scores = (
            jnp.einsum("qhe,khe->hqk", q_part, k_part, preferred_element_type=jnp.float32) * scale
            + bias
        )
        d_weights = jnp.einsum("qhe,khe->hqk", d_part, v_part, preferred_element_type=jnp.float32)
        d_scores = jnp.where(allowed[None], d_weights * silu_grad(scores), 0.0)
        rounded = d_scores.astype(jnp.bfloat16)
        result = ()
        if want_query:
            d_query = (
                jnp.einsum("hqk,khe->qhe", rounded, k_part, preferred_element_type=jnp.float32)
                * scale
            )
            d_table = table_grad(d_scores, pos_bucket, time_gap, pos_count, time_count)
            result = result + (d_query.reshape(rows, width), d_table)
        if want_keys:
            weights = jnp.where(allowed[None], jax.nn.silu(scores), 0.0).astype(jnp.bfloat16)
            d_key = (
                jnp.einsum("hqk,qhe->khe", rounded, q_part, preferred_element_type=jnp.float32)
                * scale
            )
            d_value = jnp.einsum(
                "hqk,qhe->khe", weights, d_part, preferred_element_type=jnp.float32
            )
            result = result + (d_key.reshape(rows, width), d_value.reshape(rows, width))
        return result

    d_query, d_table, d_key, d_value = grad_pair(
        query_grad, own_time, myself, keys_values, own_time, myself, True, True
    )

    def query_side(carry, inputs):
        dq_sum, table_sum = carry
        kv_block, key_time, step = inputs
        key_src = (myself - step) % count
        part = grad_pair(query_grad, own_time, myself, kv_block, key_time, key_src, True, False)
        return ((dq_sum + part[0], table_sum + part[1]), None)

    (d_query, d_table), _ = lax.scan(query_side, (d_query, d_table), (kept[0], kept[1], steps))

    def key_side(carry, step):
        dk_sum, dv_sum, qdo_block, query_time = carry
        qdo_block, query_time = shifted((qdo_block, query_time), "ctx", -1)
        query_src = (myself + step) % count
        part = grad_pair(
            qdo_block, query_time, query_src, keys_values, own_time, myself, False, True
        )
        return ((dk_sum + part[0], dv_sum + part[1], qdo_block, query_time), None)

    (d_key, d_value, _, _), _ = lax.scan(key_side, (d_key, d_value, query_grad, own_time), steps)
    grads = jnp.concatenate([d_u, d_value, d_query, d_key], axis=1)
    d_pre = (grads * silu_grad(pre.astype(jnp.float32))).astype(jnp.bfloat16)
    weight_part = lax.psum_scatter(
        lax.dot_general(hidden, cot, (((0,), (0,)), ((), ())), preferred_element_type=jnp.float32),
        ("dp", "ctx"),
        scatter_dimension=0,
        tiled=True,
    )
    gain_total, pos_total, time_total = lax.psum(
        (gain_product, d_table[:, :pos_count], d_table[:, pos_count:]), ("dp", "ctx")
    )
    return (output[None], d_pre[None], weight_part, gain_total, pos_total, time_total)


def solution(mesh):
    in_specs = (
        P("dp", "ctx", None),
        P("dp", "ctx", None),
        P("dp", None),
        P("dp", "ctx"),
        P(),
        P(),
        P(),
        P(),
        P("dp", "ctx", None),
    )
    out_specs = (P("dp", "ctx", None), P("dp", "ctx", None), P(("dp", "ctx"), None), P(), P(), P())
    return jax.shard_map(body, mesh=mesh, in_specs=in_specs, out_specs=out_specs, check_vma=False)
```

profile of v0, /device:TPU:1, one launch (start us, length us, event | category | flops | bytes accessed | tf_op | source)
XLA Modules:
  0.0 1136.6 jit_solution(9354409595596678934)
XLA Ops:
  25.5 342.4 %while.57 = (s32[]{:T(128)}, f32[128,1024]{0,1:T(8,128)S(1)}, bf16[128,2048]{0,1:T(8,128)(2,1)}, s32[128]{0:T(128)S(1)}, bf16[15,128,2048]{1,2,0:T(8,128)(2,1)},...) while((s32[]{:T(128)}, f32[128,1024]{0,1:T(8,128)S(1)}, ...), condition=%wide.region_4.5_spmd.clone, body=%wide.region_2.4_spmd.clone.sunk | while | flops 77466768 | bytes 9227390 | solution.py:125
  25.7 6.9 collective-permute-start.1
  49.5 5.1 collective-permute-start.1
  71.6 5.1 collective-permute-start.1
  93.7 5.1 collective-permute-start.1
  115.8 5.3 collective-permute-start.1
  138.1 6.0 collective-permute-start.1
  161.1 6.0 collective-permute-start.1
  184.0 6.0 collective-permute-start.1
  207.0 6.0 collective-permute-start.1
  230.0 6.0 collective-permute-start.1
  253.0 6.0 collective-permute-start.1
  276.0 6.0 collective-permute-start.1
  299.0 6.0 collective-permute-start.1
  322.0 6.0 collective-permute-start.1
  345.0 6.0 collective-permute-start.1
  392.7 262.1 %while.59 = (s32[]{:T(128)}, f32[128,1024]{0,1:T(8,128)S(1)}, f32[8,32]{1,0:T(8,128)}, bf16[15,128,2048]{1,2,0:T(8,128)(2,1)}, s32[]{:T(128)}, /*index=5*/s32[8]...) while((s32[]{:T(128)}, f32[128,1024]{0,1:T(8,128)S(1)}, ...), condition=%wide.region_80.81_spmd.clone.clone, body=%wide.region_45.80_spmd.clone.clone.sunk | while | flops 120068112 | bytes 11852566 | solution.py:206
  657.1 387.7 %while.58 = (s32[]{:T(128)}, f32[128,1024]{0,1:T(8,128)}, f32[128,1024]{0,1:T(8,128)}, bf16[128,2048]{0,1:T(8,128)(2,1)S(1)}, s32[128]{0:T(128)}, /*index=5*/s32...) while((s32[]{:T(128)}, f32[128,1024]{0,1:T(8,128)}, ...), condition=%wide.region_12.13_spmd.clone.clone, body=%wide.region_9.12_spmd.clone.clone.sunk | while | flops 146151440 | bytes 15795286 | solution.py:217
  667.3 4.7 collective-permute-done.2
  693.1 5.0 collective-permute-done.2
  719.0 4.8 collective-permute-done.2
  744.9 4.7 collective-permute-done.2
  770.6 5.0 collective-permute-done.2
  822.1 5.0 collective-permute-done.2
  848.1 4.8 collective-permute-done.2
  874.0 4.8 collective-permute-done.2
  899.8 5.0 collective-permute-done.2
  925.8 4.5 collective-permute-done.2
  951.3 5.2 collective-permute-done.2
  977.5 4.8 collective-permute-done.2
  1003.3 4.9 collective-permute-done.2
  1049.1 76.4 %all-reduce = (f32[1024]{0:T(1024)}, f32[8,16]{1,0:T(8,128)}, f32[8,16]{1,0:T(8,128)}) all-reduce(f32[1024]{0:T(1024)S(1)} %copy-done.67, f32[8,16]{1,0:T(8,128)S(1)} %get-tuple-element.1369, f32[8,16]{1,0:T(8,128)S(1)} %get-tuple-element.1368), channel_id=1, replica_groups=mesh['dp'=8,'ctx'=16] {'dp','ctx'}, use_global_device_ids=true, to_apply=%region_83.84 | all-reduce | flops 1280 | bytes 10240 | tf_op jit(solution)/shard_map/psum | solution.py:226
  (2065 shorter events, 857.8 us)
Async XLA Ops:
  7.2 1122.6 %reduce-scatter.2.cloned.1.call-start = ((), (), s32[]{:S(2)}) async-start(), calls=%async_computation.1 | async-start | bytes 4227072 | tf_op jit(solution)/shard_map/reduce_scatter | solution.py:220
  25.7 12.5 %collective-permute-start.1 = (s32[128]{0:T(128)S(1)}, s32[128]{0:T(128)S(1)}, u32[]{:S(2)}, u32[]{:S(2)}) collective-permute-start(s32[128]{0:T(128)S(1)} %get-tuple-element.2177), channel_id=1, source_target_pairs={{0,1},{1,2},{2,3},{3,4},{4,5},{5,6},{6,7},{7,8},{8,9},{9,10},{10,1... | collective-permute-start | bytes 1544 | tf_op jit(solution)/shard_map/while/body/eval_jaxpr/ppermute | solution.py:15
  49.5 10.7 collective-permute-start.1
  71.6 10.7 collective-permute-start.1
  93.7 10.7 collective-permute-start.1
  115.8 10.9 collective-permute-start.1
  138.1 11.6 %collective-permute-start.1 = (s32[128]{0:T(128)S(1)}, s32[128]{0:T(128)S(1)}, u32[]{:S(2)}, u32[]{:S(2)}) collective-permute-start(s32[128]{0:T(128)S(1)} %get-tuple-element.2177), channel_id=1, source_target_pairs={{0,1},{1,2},{2,3},{3,4},{4,5},{5,6},{6,7},{7,8},{8,9},{9,10},{10,1... | collective-permute-start | bytes 1544 | tf_op jit(solution)/shard_map/while/body/eval_jaxpr/ppermute | solution.py:15
  161.1 11.6 %collective-permute-start.1 = (s32[128]{0:T(128)S(1)}, s32[128]{0:T(128)S(1)}, u32[]{:S(2)}, u32[]{:S(2)}) collective-permute-start(s32[128]{0:T(128)S(1)} %get-tuple-element.2177), channel_id=1, source_target_pairs={{0,1},{1,2},{2,3},{3,4},{4,5},{5,6},{6,7},{7,8},{8,9},{9,10},{10,1... | collective-permute-start | bytes 1544 | tf_op jit(solution)/shard_map/while/body/eval_jaxpr/ppermute | solution.py:15
  184.0 11.6 %collective-permute-start.1 = (s32[128]{0:T(128)S(1)}, s32[128]{0:T(128)S(1)}, u32[]{:S(2)}, u32[]{:S(2)}) collective-permute-start(s32[128]{0:T(128)S(1)} %get-tuple-element.2177), channel_id=1, source_target_pairs={{0,1},{1,2},{2,3},{3,4},{4,5},{5,6},{6,7},{7,8},{8,9},{9,10},{10,1... | collective-permute-start | bytes 1544 | tf_op jit(solution)/shard_map/while/body/eval_jaxpr/ppermute | solution.py:15
  207.0 11.6 %collective-permute-start.1 = (s32[128]{0:T(128)S(1)}, s32[128]{0:T(128)S(1)}, u32[]{:S(2)}, u32[]{:S(2)}) collective-permute-start(s32[128]{0:T(128)S(1)} %get-tuple-element.2177), channel_id=1, source_target_pairs={{0,1},{1,2},{2,3},{3,4},{4,5},{5,6},{6,7},{7,8},{8,9},{9,10},{10,1... | collective-permute-start | bytes 1544 | tf_op jit(solution)/shard_map/while/body/eval_jaxpr/ppermute | solution.py:15
  230.0 11.6 %collective-permute-start.1 = (s32[128]{0:T(128)S(1)}, s32[128]{0:T(128)S(1)}, u32[]{:S(2)}, u32[]{:S(2)}) collective-permute-start(s32[128]{0:T(128)S(1)} %get-tuple-element.2177), channel_id=1, source_target_pairs={{0,1},{1,2},{2,3},{3,4},{4,5},{5,6},{6,7},{7,8},{8,9},{9,10},{10,1... | collective-permute-start | bytes 1544 | tf_op jit(solution)/shard_map/while/body/eval_jaxpr/ppermute | solution.py:15
  236.0 9.0 collective-permute-start
  253.0 11.6 %collective-permute-start.1 = (s32[128]{0:T(128)S(1)}, s32[128]{0:T(128)S(1)}, u32[]{:S(2)}, u32[]{:S(2)}) collective-permute-start(s32[128]{0:T(128)S(1)} %get-tuple-element.2177), channel_id=1, source_target_pairs={{0,1},{1,2},{2,3},{3,4},{4,5},{5,6},{6,7},{7,8},{8,9},{9,10},{10,1... | collective-permute-start | bytes 1544 | tf_op jit(solution)/shard_map/while/body/eval_jaxpr/ppermute | solution.py:15
  276.0 11.6 %collective-permute-start.1 = (s32[128]{0:T(128)S(1)}, s32[128]{0:T(128)S(1)}, u32[]{:S(2)}, u32[]{:S(2)}) collective-permute-start(s32[128]{0:T(128)S(1)} %get-tuple-element.2177), channel_id=1, source_target_pairs={{0,1},{1,2},{2,3},{3,4},{4,5},{5,6},{6,7},{7,8},{8,9},{9,10},{10,1... | collective-permute-start | bytes 1544 | tf_op jit(solution)/shard_map/while/body/eval_jaxpr/ppermute | solution.py:15
  299.0 11.6 %collective-permute-start.1 = (s32[128]{0:T(128)S(1)}, s32[128]{0:T(128)S(1)}, u32[]{:S(2)}, u32[]{:S(2)}) collective-permute-start(s32[128]{0:T(128)S(1)} %get-tuple-element.2177), channel_id=1, source_target_pairs={{0,1},{1,2},{2,3},{3,4},{4,5},{5,6},{6,7},{7,8},{8,9},{9,10},{10,1... | collective-permute-start | bytes 1544 | tf_op jit(solution)/shard_map/while/body/eval_jaxpr/ppermute | solution.py:15
  322.0 11.6 %collective-permute-start.1 = (s32[128]{0:T(128)S(1)}, s32[128]{0:T(128)S(1)}, u32[]{:S(2)}, u32[]{:S(2)}) collective-permute-start(s32[128]{0:T(128)S(1)} %get-tuple-element.2177), channel_id=1, source_target_pairs={{0,1},{1,2},{2,3},{3,4},{4,5},{5,6},{6,7},{7,8},{8,9},{9,10},{10,1... | collective-permute-start | bytes 1544 | tf_op jit(solution)/shard_map/while/body/eval_jaxpr/ppermute | solution.py:15
  345.0 11.6 %collective-permute-start.1 = (s32[128]{0:T(128)S(1)}, s32[128]{0:T(128)S(1)}, u32[]{:S(2)}, u32[]{:S(2)}) collective-permute-start(s32[128]{0:T(128)S(1)} %get-tuple-element.2177), channel_id=1, source_target_pairs={{0,1},{1,2},{2,3},{3,4},{4,5},{5,6},{6,7},{7,8},{8,9},{9,10},{10,1... | collective-permute-start | bytes 1544 | tf_op jit(solution)/shard_map/while/body/eval_jaxpr/ppermute | solution.py:15
  659.6 12.5 %collective-permute-start.2 = (bf16[128,2048]{0,1:T(8,128)(2,1)S(1)}, bf16[128,2048]{0,1:T(8,128)(2,1)S(1)}, u32[]{:S(2)}, u32[]{:S(2)}) collective-permute-start(bf16[128,2048]{0,1:T(8,128)(2,1)S(1)} %get-tuple-element.2236), channel_id=1, source_target_pairs={{1,0},{2,1},{3,2},{4,3},{5,4},{6,5},{7,6},{8,7},{9,8},{10,9},{11,1... | collective-permute-start | bytes 1572872 | tf_op jit(solution)/shard_map/while/body/eval_jaxpr/ppermute | solution.py:15
  685.3 12.7 %collective-permute-start.2 = (bf16[128,2048]{0,1:T(8,128)(2,1)S(1)}, bf16[128,2048]{0,1:T(8,128)(2,1)S(1)}, u32[]{:S(2)}, u32[]{:S(2)}) collective-permute-start(bf16[128,2048]{0,1:T(8,128)(2,1)S(1)} %get-tuple-element.2236), channel_id=1, source_target_pairs={{1,0},{2,1},{3,2},{4,3},{5,4},{6,5},{7,6},{8,7},{9,8},{10,9},{11,1... | collective-permute-start | bytes 1572872 | tf_op jit(solution)/shard_map/while/body/eval_jaxpr/ppermute | solution.py:15
  711.3 12.6 %collective-permute-start.2 = (bf16[128,2048]{0,1:T(8,128)(2,1)S(1)}, bf16[128,2048]{0,1:T(8,128)(2,1)S(1)}, u32[]{:S(2)}, u32[]{:S(2)}) collective-permute-start(bf16[128,2048]{0,1:T(8,128)(2,1)S(1)} %get-tuple-element.2236), channel_id=1, source_target_pairs={{1,0},{2,1},{3,2},{4,3},{5,4},{6,5},{7,6},{8,7},{9,8},{10,9},{11,1... | collective-permute-start | bytes 1572872 | tf_op jit(solution)/shard_map/while/body/eval_jaxpr/ppermute | solution.py:15
  737.1 12.5 %collective-permute-start.2 = (bf16[128,2048]{0,1:T(8,128)(2,1)S(1)}, bf16[128,2048]{0,1:T(8,128)(2,1)S(1)}, u32[]{:S(2)}, u32[]{:S(2)}) collective-permute-start(bf16[128,2048]{0,1:T(8,128)(2,1)S(1)} %get-tuple-element.2236), channel_id=1, source_target_pairs={{1,0},{2,1},{3,2},{4,3},{5,4},{6,5},{7,6},{8,7},{9,8},{10,9},{11,1... | collective-permute-start | bytes 1572872 | tf_op jit(solution)/shard_map/while/body/eval_jaxpr/ppermute | solution.py:15
  762.9 12.8 %collective-permute-start.2 = (bf16[128,2048]{0,1:T(8,128)(2,1)S(1)}, bf16[128,2048]{0,1:T(8,128)(2,1)S(1)}, u32[]{:S(2)}, u32[]{:S(2)}) collective-permute-start(bf16[128,2048]{0,1:T(8,128)(2,1)S(1)} %get-tuple-element.2236), channel_id=1, source_target_pairs={{1,0},{2,1},{3,2},{4,3},{5,4},{6,5},{7,6},{8,7},{9,8},{10,9},{11,1... | collective-permute-start | bytes 1572872 | tf_op jit(solution)/shard_map/while/body/eval_jaxpr/ppermute | solution.py:15
  788.9 12.2 %collective-permute-start.2 = (bf16[128,2048]{0,1:T(8,128)(2,1)S(1)}, bf16[128,2048]{0,1:T(8,128)(2,1)S(1)}, u32[]{:S(2)}, u32[]{:S(2)}) collective-permute-start(bf16[128,2048]{0,1:T(8,128)(2,1)S(1)} %get-tuple-element.2236), channel_id=1, source_target_pairs={{1,0},{2,1},{3,2},{4,3},{5,4},{6,5},{7,6},{8,7},{9,8},{10,9},{11,1... | collective-permute-start | bytes 1572872 | tf_op jit(solution)/shard_map/while/body/eval_jaxpr/ppermute | solution.py:15
  814.3 12.8 %collective-permute-start.2 = (bf16[128,2048]{0,1:T(8,128)(2,1)S(1)}, bf16[128,2048]{0,1:T(8,128)(2,1)S(1)}, u32[]{:S(2)}, u32[]{:S(2)}) collective-permute-start(bf16[128,2048]{0,1:T(8,128)(2,1)S(1)} %get-tuple-element.2236), channel_id=1, source_target_pairs={{1,0},{2,1},{3,2},{4,3},{5,4},{6,5},{7,6},{8,7},{9,8},{10,9},{11,1... | collective-permute-start | bytes 1572872 | tf_op jit(solution)/shard_map/while/body/eval_jaxpr/ppermute | solution.py:15
  840.4 12.6 %collective-permute-start.2 = (bf16[128,2048]{0,1:T(8,128)(2,1)S(1)}, bf16[128,2048]{0,1:T(8,128)(2,1)S(1)}, u32[]{:S(2)}, u32[]{:S(2)}) collective-permute-start(bf16[128,2048]{0,1:T(8,128)(2,1)S(1)} %get-tuple-element.2236), channel_id=1, source_target_pairs={{1,0},{2,1},{3,2},{4,3},{5,4},{6,5},{7,6},{8,7},{9,8},{10,9},{11,1... | collective-permute-start | bytes 1572872 | tf_op jit(solution)/shard_map/while/body/eval_jaxpr/ppermute | solution.py:15
  866.2 12.5 %collective-permute-start.2 = (bf16[128,2048]{0,1:T(8,128)(2,1)S(1)}, bf16[128,2048]{0,1:T(8,128)(2,1)S(1)}, u32[]{:S(2)}, u32[]{:S(2)}) collective-permute-start(bf16[128,2048]{0,1:T(8,128)(2,1)S(1)} %get-tuple-element.2236), channel_id=1, source_target_pairs={{1,0},{2,1},{3,2},{4,3},{5,4},{6,5},{7,6},{8,7},{9,8},{10,9},{11,1... | collective-permute-start | bytes 1572872 | tf_op jit(solution)/shard_map/while/body/eval_jaxpr/ppermute | solution.py:15
  892.0 12.8 %collective-permute-start.2 = (bf16[128,2048]{0,1:T(8,128)(2,1)S(1)}, bf16[128,2048]{0,1:T(8,128)(2,1)S(1)}, u32[]{:S(2)}, u32[]{:S(2)}) collective-permute-start(bf16[128,2048]{0,1:T(8,128)(2,1)S(1)} %get-tuple-element.2236), channel_id=1, source_target_pairs={{1,0},{2,1},{3,2},{4,3},{5,4},{6,5},{7,6},{8,7},{9,8},{10,9},{11,1... | collective-permute-start | bytes 1572872 | tf_op jit(solution)/shard_map/while/body/eval_jaxpr/ppermute | solution.py:15
  918.0 12.2 %collective-permute-start.2 = (bf16[128,2048]{0,1:T(8,128)(2,1)S(1)}, bf16[128,2048]{0,1:T(8,128)(2,1)S(1)}, u32[]{:S(2)}, u32[]{:S(2)}) collective-permute-start(bf16[128,2048]{0,1:T(8,128)(2,1)S(1)} %get-tuple-element.2236), channel_id=1, source_target_pairs={{1,0},{2,1},{3,2},{4,3},{5,4},{6,5},{7,6},{8,7},{9,8},{10,9},{11,1... | collective-permute-start | bytes 1572872 | tf_op jit(solution)/shard_map/while/body/eval_jaxpr/ppermute | solution.py:15
  943.5 12.9 %collective-permute-start.2 = (bf16[128,2048]{0,1:T(8,128)(2,1)S(1)}, bf16[128,2048]{0,1:T(8,128)(2,1)S(1)}, u32[]{:S(2)}, u32[]{:S(2)}) collective-permute-start(bf16[128,2048]{0,1:T(8,128)(2,1)S(1)} %get-tuple-element.2236), channel_id=1, source_target_pairs={{1,0},{2,1},{3,2},{4,3},{5,4},{6,5},{7,6},{8,7},{9,8},{10,9},{11,1... | collective-permute-start | bytes 1572872 | tf_op jit(solution)/shard_map/while/body/eval_jaxpr/ppermute | solution.py:15
  969.7 12.6 %collective-permute-start.2 = (bf16[128,2048]{0,1:T(8,128)(2,1)S(1)}, bf16[128,2048]{0,1:T(8,128)(2,1)S(1)}, u32[]{:S(2)}, u32[]{:S(2)}) collective-permute-start(bf16[128,2048]{0,1:T(8,128)(2,1)S(1)} %get-tuple-element.2236), channel_id=1, source_target_pairs={{1,0},{2,1},{3,2},{4,3},{5,4},{6,5},{7,6},{8,7},{9,8},{10,9},{11,1... | collective-permute-start | bytes 1572872 | tf_op jit(solution)/shard_map/while/body/eval_jaxpr/ppermute | solution.py:15
  995.6 12.6 %collective-permute-start.2 = (bf16[128,2048]{0,1:T(8,128)(2,1)S(1)}, bf16[128,2048]{0,1:T(8,128)(2,1)S(1)}, u32[]{:S(2)}, u32[]{:S(2)}) collective-permute-start(bf16[128,2048]{0,1:T(8,128)(2,1)S(1)} %get-tuple-element.2236), channel_id=1, source_target_pairs={{1,0},{2,1},{3,2},{4,3},{5,4},{6,5},{7,6},{8,7},{9,8},{10,9},{11,1... | collective-permute-start | bytes 1572872 | tf_op jit(solution)/shard_map/while/body/eval_jaxpr/ppermute | solution.py:15
  1021.5 12.0 %collective-permute-start.2 = (bf16[128,2048]{0,1:T(8,128)(2,1)S(1)}, bf16[128,2048]{0,1:T(8,128)(2,1)S(1)}, u32[]{:S(2)}, u32[]{:S(2)}) collective-permute-start(bf16[128,2048]{0,1:T(8,128)(2,1)S(1)} %get-tuple-element.2236), channel_id=1, source_target_pairs={{1,0},{2,1},{3,2},{4,3},{5,4},{6,5},{7,6},{8,7},{9,8},{10,9},{11,1... | collective-permute-start | bytes 1572872 | tf_op jit(solution)/shard_map/while/body/eval_jaxpr/ppermute | solution.py:15
  (374 other events, 2081.9 us)
Sparse Core Ops, SparseCore 0:
  376.4 641.8 reduce-scatter.1
where the time goes:
time: 1150 us; the launch traced here: 1140 us
  local copies, waits for them, and re-layouts  324 us (28%)
  matrix products  244 us (21%)
  other arithmetic  194 us (17%)
  starting transfers between devices  175 us (15%)
  blocking collectives  76.4 us (7%)
  waiting for transfers between devices  72 us (6%)
  loops' own time  36.7 us (3%)
  between operations  14.9 us (1%)
    ppermute x60, starting transfers between devices, shifted(): lax.ppermute(value, axis, [(source, source + steps) for source in range(f...  175 us
    another operation x528, local copies, waits for them, and re-layouts, table_grad(): return jnp.stack(columns, axis=1)  83.7 us
    dot_general x30, matrix products, grad_pair(): jnp.einsum('qhe,khe->hqk', q_part, k_part, preferred_element_type=jnp.flo...  76.4 us
    psum x1, blocking collectives, body(): lax.psum((gain_product, d_table[:, :pos_count], d_table[:, pos_count:]),...  76.4 us
    ppermute x60, waiting for transfers between devices, shifted(): lax.ppermute(value, axis, [(source, source + steps) for source in range(f...  72 us
    dot_general x16, matrix products, attend(): jnp.einsum('hqk,khe->qhe', weights, split_heads(kv_block[:, width:]), pre...  64.6 us
    while x600, local copies, waits for them, and re-layouts  58.6 us
    eq x46, other arithmetic, bias_of(): time_gap[None] == bucket  42.3 us
  transfers between devices with their start and end apart: 61, of which 15 were waited for; matrix products, arithmetic and copies ran while one was open for 53% of the time, Pallas kernels for 0%

commit v1 on v0

v1 whole, which is shorter than its diff:
```python
import jax
import jax.numpy as jnp
from jax import lax
from jax.experimental import pallas as pl
from jax.experimental.pallas import tpu as pltpu
from jax.sharding import PartitionSpec as P

MESH = pl.DeviceIdType.MESH
F32 = jnp.float32
BF16 = jnp.bfloat16

HEADS = 8
EPS = 1e-05
ROWS = 128
CHIPS = 8
SPAN = 9
WIN = SPAN * ROWS
PAD = SPAN - 1
WIDTH = HEADS * ROWS
BUCKETS = 16
FAR = 131072.0
SCALE = ROWS ** (-0.5)

KEY, VAL, TIM, QUE, DNO, END = 0, 128, 256, 272, 400, 528
CHUNKS = [(0, 256), (256, 256), (512, 256), (768, 256), (1024, 128)]

NT = (((1,), (1,)), ((), ()))
TN = (((0,), (0,)), ((), ()))
NN = (((1,), (0,)), ((), ()))


def dot(a, b, dims=NN):
    return lax.dot_general(a, b, dims, preferred_element_type=F32)


def exact_dot(a, b, dims=NN):
    return lax.dot_general(
        a, b, dims, preferred_element_type=F32, precision=lax.Precision.HIGHEST
    )


def silu_half(x):
    return x * (1.0 + jnp.tanh(x))


def silu_grad_half(x):
    t = jnp.tanh(x)
    a = 1.0 + t
    return 0.5 * (a + x * a * (1.0 - t))


def columns(h):
    return pl.ds(pl.multiple_of(h * ROWS, ROWS), ROWS)


def kernel(
    uvqk, resid, lens, times, ptab, ttab, gain, wout, cot,
    out, dpre, dwo, dgain, dpos, dtime,
    sb, rb, cot2, dh, kext, vall, aext, wa, pbias, wsave, fsave,
    att_t, pn_t, gcol, att_s, att_r, stats, comb, dout, hid, hid_s, hid2,
    ds_s, ds_r, e_s, e_r, diag, dkv, pacc, tmat, gacc, mq_s, mq_r, xs, xr, mk_s, mk_r,
    tab, tab1, tab2,
    loc_sem, m1s, m1r, m2s, m2r, fws, fwr, sib_s, sib_r, ats, atr, sts, str_,
    d1s, d1r, d2s, d2r, qs, qr, ks, kr, t1s, t1r, t2s, t2r,
):
    dp = lax.axis_index("dp")
    me = lax.axis_index("ctx")
    c = me // 2
    r = me % 2
    y = dp // 2
    zl = dp % 2
    sib = 2 * c + (1 - r)

    def remote(src, dst, ssem, rsem, to):
        return pltpu.make_async_remote_copy(
            src_ref=src, dst_ref=dst, send_sem=ssem, recv_sem=rsem, device_id=to,
            device_id_type=MESH,
        )

    barrier = pltpu.get_barrier_semaphore()

    def greet(j, _):
        pl.semaphore_signal(
            barrier, inc=1, device_id=(2 * y + (zl + j // 16) % 2, (me + j % 16) % 16),
            device_id_type=MESH,
        )
        return 0

    lax.fori_loop(1, 32, greet, 0)

    def greet_far(j, _):
        pl.semaphore_signal(
            barrier, inc=1, device_id=(2 * ((y + 1 + j // 2) % 4) + j % 2, me),
            device_id_type=MESH,
        )
        return 0

    lax.fori_loop(0, 6, greet_far, 0)

    time_rows = jnp.broadcast_to(times[...].astype(F32), (16, ROWS)).astype(BF16)

    def activate(h, _):
        for group, where in ((3, KEY), (1, VAL), (2, QUE)):
            x = 0.5 * uvqk[:, columns(group * HEADS + h)].astype(F32)
            sb[h, pl.ds(where, ROWS), :] = silu_half(x).astype(BF16)
        sb[h, pl.ds(TIM, 16), :] = time_rows
        return 0

    lax.fori_loop(0, HEADS, activate, 0)
    pl.semaphore_wait(barrier, 37)

    def m1(k):
        to = (c + k) % CHIPS
        return remote(
            sb.at[to, pl.ds(0, DNO)], rb.at[me, pl.ds(0, DNO)], m1s.at[k], m1r.at[k],
            (dp, 2 * to + r),
        )

    def m2(k):
        to = (c + k) % CHIPS
        return remote(
            sb.at[to, pl.ds(DNO, ROWS)], rb.at[me, pl.ds(DNO, ROWS)], m2s.at[k], m2r.at[k],
            (dp, 2 * to + r),
        )

    own_fw = remote(
        sb.at[c, pl.ds(0, QUE)], rb.at[me, pl.ds(0, QUE)], fws.at[0], fwr.at[0], (dp, sib)
    )

    def fw(k):
        block = 2 * ((c + CHIPS - k) % CHIPS) + r
        return remote(
            rb.at[block, pl.ds(0, QUE)], rb.at[block, pl.ds(0, QUE)], fws.at[k], fwr.at[k],
            (dp, sib),
        )

    cot_copy = remote(cot, cot2.at[pl.ds(ROWS, ROWS)], sib_s.at[0], sib_r.at[0], (dp, sib))

    for k in range(1, CHIPS):
        m1(k).start()
    own_fw.start()
    cot_copy.start()
    own1 = pltpu.make_async_copy(
        sb.at[c, pl.ds(0, DNO)], rb.at[me, pl.ds(0, DNO)], loc_sem.at[0]
    )
    own1.start()

    dh[...] = dot(cot[...], wout[...], NT)

    def d_normed(h, _):
        x = 0.5 * uvqk[:, columns(h)].astype(F32)
        u = silu_half(x).astype(BF16).astype(F32)
        sb[h, pl.ds(DNO, ROWS), :] = (dh[:, columns(h)] * u).astype(BF16)
        return 0

    lax.fori_loop(0, HEADS, d_normed, 0)
    for k in range(1, CHIPS):
        m2(k).start()
    own2 = pltpu.make_async_copy(
        sb.at[c, pl.ds(DNO, ROWS)], rb.at[me, pl.ds(DNO, ROWS)], loc_sem.at[1]
    )
    own2.start()

    cot2[pl.ds(0, ROWS), :] = cot[...]
    kext[pl.ds(0, PAD * ROWS), :] = jnp.zeros((PAD * ROWS, 2 * ROWS), BF16)
    vall[pl.ds(0, PAD * ROWS), :] = jnp.zeros((PAD * ROWS, ROWS), BF16)
    dkv[...] = jnp.zeros_like(dkv)
    pacc[...] = jnp.zeros_like(pacc)
    tmat[...] = jnp.zeros_like(tmat)
    gacc[...] = jnp.zeros_like(gacc)
    diag[...] = jnp.zeros_like(diag)
    gcol[...] = jnp.transpose(jnp.broadcast_to(gain[:, columns(c)], (ROWS, ROWS)))

    sub = lax.broadcasted_iota(jnp.int32, (ROWS, ROWS), 0)
    lane = lax.broadcasted_iota(jnp.int32, (ROWS, ROWS), 1)
    sub_s = lax.broadcasted_iota(jnp.int32, (BUCKETS, ROWS), 0)
    lane_s = lax.broadcasted_iota(jnp.int32, (BUCKETS, ROWS), 1)
    spread = jnp.abs(sub_s - lane_s % BUCKETS)
    table = jnp.zeros((BUCKETS, ROWS), F32)
    for b in range(BUCKETS):
        table = jnp.where(spread == b, ttab[c, b] * (1.0 / SCALE), table)
    part = table.astype(BF16).astype(F32)
    rest = table - part
    middle = rest.astype(BF16).astype(F32)
    table = jnp.where(
        lane_s < 16, part, jnp.where(lane_s < 32, middle, jnp.where(lane_s < 48, rest - middle, 0.0))
    )
    wa[...] = jnp.where(
        (sub >= 48) & (sub < 56) & (lane >= 48) & (lane < 56) & (sub != lane), -FAR, 0.0
    ).astype(BF16)
    wa[pl.ds(0, BUCKETS), :] = table.astype(BF16)

    for w in range(SPAN):
        gap = PAD * ROWS - w * ROWS + sub - lane
        bucket = jnp.minimum(jnp.maximum(gap, 0) // 64, BUCKETS - 1)
        tile = jnp.zeros((ROWS, ROWS), F32)
        low = 2 * (PAD - w) - 2
        for b in range(max(low, 0), min(low + 4, BUCKETS)):
            tile = jnp.where(bucket == b, 0.5 * ptab[c, b], tile)
        if low + 3 >= BUCKETS:
            tile = jnp.where(bucket == BUCKETS - 1, 0.5 * ptab[c, BUCKETS - 1], tile)
        if w == SPAN - 1:
            tile = jnp.where(gap < 0, -4096.0, tile)
        pbias[:, pl.ds(w * ROWS, ROWS)] = tile

    for k in range(1, CHIPS):
        m1(k).wait_recv()
        fw(k).start()
    own1.wait()
    own_fw.wait_recv()
    for k in range(1, CHIPS):
        fw(k).wait_recv()

    ends = [lens[0, 0]]
    for k in range(1, 7):
        ends.append(ends[-1] + lens[0, k])

    def features(block, _):
        t = rb[block, pl.ds(TIM, 16), :].astype(F32)[0:1, :]
        where = block * ROWS + lax.broadcasted_iota(jnp.int32, (1, ROWS), 1)
        user = jnp.zeros((1, ROWS), jnp.int32)
        for end in ends:
            user = user + (where >= end).astype(jnp.int32)
        index = jnp.where(sub < 48, sub % BUCKETS, sub - 48)
        value = jnp.where(sub < 48, t.astype(jnp.int32), jnp.where(sub < 56, user, -1))
        hot = jnp.where(index == value, 1.0, 0.0)
        at = pl.ds(pl.multiple_of((block + PAD) * ROWS, ROWS), ROWS)
        kext[at, pl.ds(ROWS, ROWS)] = jnp.transpose(hot).astype(BF16)
        kext[at, pl.ds(0, ROWS)] = rb[block, pl.ds(KEY, ROWS), :]
        vall[at, :] = rb[block, pl.ds(VAL, ROWS), :]
        return 0

    lax.fori_loop(0, 2 * CHIPS, features, 0)

    for k in range(1, CHIPS):
        m2(k).wait_recv()
    own2.wait()

    def att_copy(k):
        t = (c + k) % CHIPS
        return remote(att_s.at[t], att_r.at[c], ats.at[k], atr.at[k], (dp, 2 * t + r))

    def window(b, first, size):
        return pl.ds(pl.multiple_of(b * ROWS + first, ROWS), size)

    def forward(k, _):
        t = (c + k) % CHIPS
        b = 2 * t + r
        own = pl.ds(pl.multiple_of((b + PAD) * ROWS, ROWS), ROWS)
        feat = dot(kext[own, pl.ds(ROWS, ROWS)], wa[...]).astype(BF16)
        query = jnp.concatenate([rb[b, pl.ds(QUE, ROWS), :], feat], axis=1)
        total = jnp.zeros((ROWS, ROWS), F32)
        for first, size in CHUNKS:
            x = dot(query, kext[window(b, first, size), :], NT) * (0.5 * SCALE)
            x = x + pbias[:, pl.ds(first, size)]
            th = jnp.tanh(x)
            a = 1.0 + th
            w = x * a
            fsave[t, :, pl.ds(first, size)] = a + w * (1.0 - th)
            w = w.astype(BF16)
            wsave[t, :, pl.ds(first, size)] = w
            total = total + dot(w, vall[window(b, first, size), :])
        att_s[t] = total.astype(BF16)

        @pl.when(k > 0)
        def _():
            att_copy(k).start()

        tr = jnp.transpose(total)
        att_t[t] = tr
        pn = jnp.transpose(rb[b, pl.ds(DNO, ROWS), :].astype(F32))
        pn_t[t] = pn
        g = pn * gcol[...]
        mean = jnp.sum(tr, axis=0, keepdims=True) * (1.0 / ROWS)
        dev = tr - mean
        row = pl.ds(t, 1)
        stats[c, 0, row, :] = mean
        stats[c, 1, row, :] = jnp.sum(dev * dev, axis=0, keepdims=True)
        stats[c, 2, row, :] = jnp.sum(dev * g, axis=0, keepdims=True)
        stats[c, 3, row, :] = jnp.sum(g, axis=0, keepdims=True)
        return 0

    lax.fori_loop(0, CHIPS, forward, 0)

    def stat_copy(k):
        to = (c + k) % CHIPS
        return remote(stats.at[c], stats.at[c], sts.at[k], str_.at[k], (dp, 2 * to + r))

    def stat_recv(k):
        source = (c + CHIPS - k) % CHIPS
        return remote(
            stats.at[source], stats.at[source], sts.at[k], str_.at[k], (dp, 2 * source + r)
        )

    for k in range(1, CHIPS):
        stat_copy(k).start()
    att_r[c] = att_s[c]
    for k in range(1, CHIPS):
        stat_recv(k).wait_recv()

    mean = stats[0, 0]
    for h in range(1, HEADS):
        mean = mean + stats[h, 0]
    mean = mean * (1.0 / HEADS)
    spread2 = jnp.zeros((CHIPS, ROWS), F32)
    cross = jnp.zeros((CHIPS, ROWS), F32)
    gsum = jnp.zeros((CHIPS, ROWS), F32)
    for h in range(HEADS):
        off = stats[h, 0] - mean
        spread2 = spread2 + (stats[h, 1] + ROWS * (off * off))
        cross = cross + (stats[h, 2] + off * stats[h, 3])
        gsum = gsum + stats[h, 3]
    inv = lax.rsqrt(spread2 * (1.0 / WIDTH) + EPS)
    comb[0] = mean
    comb[1] = inv
    comb[2] = gsum * (1.0 / WIDTH)
    comb[3] = cross * inv * (1.0 / WIDTH)

    def d_attended(t, _):
        row = pl.ds(t, 1)
        inv_t = comb[1, row, :]
        xhat = (att_t[t] - comb[0, row, :]) * inv_t
        pn = pn_t[t]
        gacc[...] += pn * xhat
        d = inv_t * (pn * gcol[...] - comb[2, row, :] - xhat * comb[3, row, :])
        dout[t] = (0.5 * jnp.transpose(d)).astype(BF16)
        return 0

    lax.fori_loop(0, CHIPS, d_attended, 0)

    mine = pl.ds(c, 1)
    mean_c = jnp.transpose(jnp.broadcast_to(comb[0, mine, :], (ROWS, ROWS)))
    inv_c = jnp.transpose(jnp.broadcast_to(comb[1, mine, :], (ROWS, ROWS)))
    for k in range(1, CHIPS):
        att_copy(k).wait_recv()

    def rows_of(h, _):
        normed = (att_r[h].astype(F32) - mean_c) * inv_c * gain[:, columns(h)]
        x = 0.5 * uvqk[:, columns(h)].astype(F32)
        t = jnp.tanh(x)
        a = 1.0 + t
        s = x * a
        hidden = (normed * s.astype(BF16).astype(F32)).astype(BF16)
        hid[:, columns(h)] = hidden
        hid_s[h % 2, h // 2] = hidden
        d_u = dh[:, columns(h)] * normed
        dpre[:, columns(h)] = (d_u * (0.5 * (a + s * (1.0 - t)))).astype(BF16)
        return 0

    lax.fori_loop(0, HEADS, rows_of, 0)
    hid_copy = remote(
        hid_s.at[1 - r], hid2.at[:, pl.ds(ROWS, ROWS), :], sib_s.at[1], sib_r.at[1], (dp, sib)
    )
    hid_copy.start()
    hid2[:, pl.ds(0, ROWS), :] = hid_s[r]
    out[...] = (resid[...].astype(F32) + dot(hid[...], wout[...])).astype(BF16)
    cot_copy.wait_recv()
    hid_copy.wait_recv()

    def d1(k):
        to = (y + k) % 4
        return remote(ds_s.at[to], ds_r.at[y], d1s.at[k], d1r.at[k], (2 * to + zl, me))

    for k in range(1, 5):
        to = (y + k) % 4
        ds_s[to] = dot(hid2[to], cot2[...], TN).astype(BF16)
        if k < 4:
            d1(k).start()

    def dq_copy(k):
        t = (c + k) % CHIPS
        return remote(mq_s.at[t], mq_r.at[c], qs.at[k], qr.at[k], (dp, 2 * t + r))

    def backward(k, _):
        t = (c + k) % CHIPS
        b = 2 * t + r
        d = dout[t]
        diag[pl.ds(0, ROWS), pl.ds(0, ROWS)] = rb[b, pl.ds(QUE, ROWS), :]
        diag[pl.ds(ROWS, ROWS), pl.ds(ROWS, ROWS)] = d
        both = diag[...]
        dq = jnp.zeros((ROWS, 2 * ROWS), F32)
        for first, size in CHUNKS:
            at = window(b, first, size)
            some = pl.ds(first, size)
            ds = dot(d, vall[at, :], NT) * fsave[t, :, some]
            pacc[:, some] += ds
            ds = ds.astype(BF16)
            dq = dq + dot(ds, kext[at, :])
            dkv[at, :] += dot(jnp.concatenate([ds, wsave[t, :, some]], axis=0), both, TN)
        mq_s[t] = (dq[:, :ROWS] * SCALE).astype(BF16)

        @pl.when(k > 0)
        def _():
            dq_copy(k).start()

        high = dq[:, ROWS:].astype(BF16)
        low = (dq[:, ROWS:] - high.astype(F32)).astype(BF16)
        own = pl.ds(pl.multiple_of((b + PAD) * ROWS, ROWS), ROWS)
        hot = kext[own, pl.ds(ROWS, ROWS)]
        tmat[...] += dot(hot, high, TN) + dot(hot, low, TN)
        return 0

    lax.fori_loop(0, CHIPS, backward, 0)

    def to_sibling(t, _):
        at = pl.ds(pl.multiple_of((2 * t + (1 - r) + PAD) * ROWS, ROWS), ROWS)
        xs[t] = dkv[at, :].astype(BF16)
        return 0

    lax.fori_loop(0, CHIPS, to_sibling, 0)
    dkv_copy = remote(xs, xr, sib_s.at[2], sib_r.at[2], (dp, sib))
    dkv_copy.start()

    sums = []
    for b in range(BUCKETS):
        total = jnp.zeros((1, ROWS), F32)
        for w in range(SPAN):
            low = 2 * (PAD - w) - 2
            if low <= b < low + 4 or (b == BUCKETS - 1 and low + 3 >= BUCKETS):
                gap = PAD * ROWS - w * ROWS + sub - lane
                bucket = jnp.minimum(jnp.maximum(gap, 0) // 64, BUCKETS - 1)
                picked = jnp.where(bucket == b, pacc[:, pl.ds(w * ROWS, ROWS)], 0.0)
                total = total + jnp.sum(picked, axis=0, keepdims=True)
        sums.append(total)
    near = tmat[pl.ds(0, BUCKETS), :]
    gap_t = jnp.where(lane_s < BUCKETS, jnp.abs(sub_s - lane_s), -1)
    for b in range(BUCKETS):
        sums.append(jnp.sum(jnp.where(gap_t == b, near, 0.0), axis=0, keepdims=True))
    ones = jnp.ones((8, ROWS), F32)
    sums = jnp.concatenate(sums + [jnp.zeros((ROWS - 2 * BUCKETS, ROWS), F32)], axis=0)
    table_sums = exact_dot(ones, sums, NT)
    gain_sums = exact_dot(ones, gacc[...], NT)
    sub8 = lax.broadcasted_iota(jnp.int32, (8, ROWS), 0)
    tab1[dp] = jnp.where(sub8 == 0, gain_sums, table_sums)

    def t1(k):
        return remote(tab1.at[dp], tab1.at[dp], t1s.at[k], t1r.at[k], ((dp + k) % 8, me))

    def t1_recv(k):
        source = (dp + 8 - k) % 8
        return remote(tab1.at[source], tab1.at[source], t1s.at[k], t1r.at[k], (source, me))

    for k in range(1, 8):
        t1(k).start()

    dkv_copy.wait_recv()

    def kv_copy(k):
        t = (c + k) % CHIPS
        return remote(mk_s.at[t], mk_r.at[c], ks.at[k], kr.at[k], (dp, 2 * t + r))

    def join(k, _):
        t = (c + k) % CHIPS
        at = pl.ds(pl.multiple_of((2 * t + r + PAD) * ROWS, ROWS), ROWS)
        total = dkv[at, :] + xr[t].astype(F32)
        mk_s[t, 0] = (total[:, :ROWS] * SCALE).astype(BF16)
        mk_s[t, 1] = (total[:, ROWS:] * 2.0).astype(BF16)

        @pl.when(k > 0)
        def _():
            kv_copy(k).start()

        return 0

    lax.fori_loop(0, CHIPS, join, 0)
    mq_r[c] = mq_s[c]
    mk_r[c] = mk_s[c]

    for k in range(1, 4):
        d1(k).wait_recv()
    ds_r[y] = ds_s[y]
    for pair in range(CHIPS):
        at = pl.ds(pair * 16, 16)
        total = ds_r[0, at, :].astype(F32)
        for k in range(1, 4):
            total = total + ds_r[k, at, :].astype(F32)
        e_s[2 * pair] = total[:8]
        e_s[2 * pair + 1] = total[8:]

    slot = zl * CHIPS + c

    def d2(j):
        to = (me + j) % 16
        return remote(e_s.at[to], e_r.at[slot], d2s.at[j], d2r.at[slot], (2 * y + r, to))

    def d2_recv(j):
        z_from = (zl + j // CHIPS) % 2
        c_from = (c + j % CHIPS) % CHIPS
        here = z_from * CHIPS + c_from
        return remote(
            e_s.at[0], e_r.at[here], d2s.at[0], d2r.at[here], (2 * y + z_from, 2 * c_from + zl)
        )

    for j in range(1, 16):
        d2(j).start()

    @pl.when(r != zl)
    def _():
        d2(0).start()

    @pl.when(r == zl)
    def _():
        e_r[slot] = e_s[me]

    for k in range(1, 8):
        t1_recv(k).wait_recv()
    total = tab1[0]
    for k in range(1, 8):
        total = total + tab1[k]
    tab2[me] = total

    def t2(k):
        return remote(tab2.at[me], tab2.at[me], t2s.at[k], t2r.at[k], (dp, (me + k) % 16))

    def t2_recv(k):
        source = (me + 16 - k) % 16
        return remote(tab2.at[source], tab2.at[source], t2s.at[k], t2r.at[k], (dp, source))

    for k in range(1, 16):
        t2(k).start()

    for k in range(1, CHIPS):
        dq_copy(k).wait_recv()
    for k in range(1, CHIPS):
        kv_copy(k).wait_recv()

    def finish(h, _):
        for group, value in ((1, mk_r[h, 1]), (2, mq_r[h]), (3, mk_r[h, 0])):
            at = columns(group * HEADS + h)
            x = 0.5 * uvqk[:, at].astype(F32)
            dpre[:, at] = (value.astype(F32) * silu_grad_half(x)).astype(BF16)
        return 0

    lax.fori_loop(0, HEADS, finish, 0)

    for k in range(1, 16):
        t2_recv(k).wait_recv()
    for h in range(HEADS):
        pair = tab2[2 * h] + tab2[2 * h + 1]
        dgain[:, pl.ds(h * ROWS, ROWS)] = pair[0:1]
        dpos[pl.ds(h, 1), :] = pair[1:2, :BUCKETS]
        dtime[pl.ds(h, 1), :] = pair[1:2, BUCKETS : 2 * BUCKETS]

    for j in range(1, 16):
        d2_recv(j).wait_recv()

    @pl.when(r != zl)
    def _():
        d2_recv(0).wait_recv()
        d2(0).wait_send()

    total = e_r[0]
    for k in range(1, 16):
        total = total + e_r[k]
    dwo[...] = total

    own_fw.wait_send()
    cot_copy.wait_send()
    hid_copy.wait_send()
    dkv_copy.wait_send()
    for k in range(1, CHIPS):
        m1(k).wait_send()
        m2(k).wait_send()
        fw(k).wait_send()
        att_copy(k).wait_send()
        stat_copy(k).wait_send()
        dq_copy(k).wait_send()
        kv_copy(k).wait_send()
        t1(k).wait_send()
    for k in range(1, 4):
        d1(k).wait_send()
    for k in range(1, 16):
        d2(k).wait_send()
        t2(k).wait_send()


def body(
    uvqk, residual, lengths, time_buckets, pos_table, time_table, output_norm_gain, w_out, cotangent
):
    vm = pl.BlockSpec(memory_space=pltpu.VMEM)
    sm = pl.BlockSpec(memory_space=pltpu.SMEM)
    tile = (ROWS, ROWS)
    dma = pltpu.SemaphoreType.DMA
    padded = (2 * CHIPS + PAD) * ROWS
    scratch = [
        pltpu.VMEM((HEADS, END, ROWS), BF16),
        pltpu.VMEM((2 * CHIPS, END, ROWS), BF16),
        pltpu.VMEM((2 * ROWS, WIDTH), BF16),
        pltpu.VMEM((ROWS, WIDTH), F32),
        pltpu.VMEM((padded, 2 * ROWS), BF16),
        pltpu.VMEM((padded, ROWS), BF16),
        pltpu.VMEM(tile, BF16),
        pltpu.VMEM(tile, BF16),
        pltpu.VMEM((ROWS, WIN), F32),
        pltpu.VMEM((CHIPS, ROWS, WIN), BF16),
        pltpu.VMEM((CHIPS, ROWS, WIN), F32),
        pltpu.VMEM((CHIPS,) + tile, F32),
        pltpu.VMEM((CHIPS,) + tile, F32),
        pltpu.VMEM(tile, F32),
        pltpu.VMEM((CHIPS,) + tile, BF16),
        pltpu.VMEM((HEADS,) + tile, BF16),
        pltpu.VMEM((HEADS, 4, CHIPS, ROWS), F32),
        pltpu.VMEM((4, CHIPS, ROWS), F32),
        pltpu.VMEM((CHIPS,) + tile, BF16),
        pltpu.VMEM((ROWS, WIDTH), BF16),
        pltpu.VMEM((2, 4) + tile, BF16),
        pltpu.VMEM((4, 2 * ROWS, ROWS), BF16),
        pltpu.VMEM((4, ROWS, WIDTH), BF16),
        pltpu.VMEM((4, ROWS, WIDTH), BF16),
        pltpu.VMEM((16, 8, WIDTH), F32),
        pltpu.VMEM((16, 8, WIDTH), F32),
        pltpu.VMEM((2 * ROWS, 2 * ROWS), BF16),
        pltpu.VMEM((padded, 2 * ROWS), F32),
        pltpu.VMEM((ROWS, WIN), F32),
        pltpu.VMEM(tile, F32),
        pltpu.VMEM(tile, F32),
        pltpu.VMEM((CHIPS,) + tile, BF16),
        pltpu.VMEM((HEADS,) + tile, BF16),
        pltpu.VMEM((CHIPS, ROWS, 2 * ROWS), BF16),
        pltpu.VMEM((CHIPS, ROWS, 2 * ROWS), BF16),
        pltpu.VMEM((CHIPS, 2) + tile, BF16),
        pltpu.VMEM((HEADS, 2) + tile, BF16),
        pltpu.VMEM((8, ROWS), F32),
        pltpu.VMEM((8, 8, ROWS), F32),
        pltpu.VMEM((16, 8, ROWS), F32),
        dma((2,)),
    ] + [
        dma((count,))
        for count in (8, 8, 8, 8, 8, 8, 3, 3, 8, 8, 8, 8, 4, 4, 16, 16, 8, 8, 8, 8, 8, 8, 16, 16)
    ]
    out, dpre, dwo, dgain, dpos, dtime = pl.pallas_call(
        kernel,
        out_shape=(
            jax.ShapeDtypeStruct((ROWS, WIDTH), BF16),
            jax.ShapeDtypeStruct((ROWS, 4 * WIDTH), BF16),
            jax.ShapeDtypeStruct((8, WIDTH), F32),
            jax.ShapeDtypeStruct((1, WIDTH), F32),
            jax.ShapeDtypeStruct((HEADS, BUCKETS), F32),
            jax.ShapeDtypeStruct((HEADS, BUCKETS), F32),
        ),
        in_specs=[vm, vm, sm, vm, sm, sm, vm, vm, vm],
        out_specs=(vm,) * 6,
        scratch_shapes=scratch,
        compiler_params=pltpu.CompilerParams(
            collective_id=0, has_side_effects=True, vmem_limit_bytes=56 * 1024 * 1024
        ),
    )(
        uvqk[0], residual[0], lengths, time_buckets, pos_table, time_table,
        output_norm_gain[None], w_out, cotangent[0],
    )
    return (out[None], dpre[None], dwo, dgain[0], dpos, dtime)


def solution(mesh):
    in_specs = (
        P("dp", "ctx", None),
        P("dp", "ctx", None),
        P("dp", None),
        P("dp", "ctx"),
        P(),
        P(),
        P(),
        P(),
        P("dp", "ctx", None),
    )
    out_specs = (P("dp", "ctx", None), P("dp", "ctx", None), P(("dp", "ctx"), None), P(), P(), P())
    return jax.shard_map(body, mesh=mesh, in_specs=in_specs, out_specs=out_specs, check_vma=False)
```

time: 1150 us -> 81.4 us (0.07); the launches traced: 1140 us -> 81.3 us
  local copies, waits for them, and re-layouts: 324 us -> 6.37 us
  matrix products: 244 us -> 0 us
  other arithmetic: 194 us -> 0 us
  starting transfers between devices: 175 us -> 0 us
  blocking collectives: 76.4 us -> 0 us
  Pallas kernels: 0 us -> 74.2 us
  waiting for transfers between devices: 72 us -> 0 us
  loops' own time: 36.7 us -> 0 us
  between operations: 14.9 us -> 0.68 us
    dot_general x114 -> x0, matrix products: 244 us -> none  [the longest x30 76.4 us: grad_pair(): jnp.einsum('qhe,khe->hqk', q_part, k_part, preferred_element_type=jnp.flo...]
    ppermute x60 -> x0, starting transfers between devices: 175 us -> none  [shifted(): lax.ppermute(value, axis, [(source, source + steps) for source in range(f...]
    another operation x528 -> x0, local copies, waits for them, and re-layouts: 83.7 us -> none  [table_grad(): return jnp.stack(columns, axis=1)]
    psum x1 -> x0, blocking collectives: 76.4 us -> none  [body(): lax.psum((gain_product, d_table[:, :pos_count], d_table[:, pos_count:]),...]
    add x137 -> x0, other arithmetic: 74.9 us -> none  [the longest x15 36.4 us: key_side(): return ((dk_sum + part[0], dv_sum + part[1], qdo_block, query_time), None)]
    pallas_call x0 -> x1, Pallas kernels: none -> 74.2 us  [body(): pl.pallas_call(kernel, out_shape=(jax.ShapeDtypeStruct((ROWS, WIDTH), BF1...]
    ppermute x60 -> x0, waiting for transfers between devices: 72 us -> none  [shifted(): lax.ppermute(value, axis, [(source, source + steps) for source in range(f...]
    while x604 -> x0, local copies, waits for them, and re-layouts: 64 us -> none
  transfers between devices with their start and end apart: 61 -> 0, of which waited for: 15 -> 0; matrix products, arithmetic and copies ran while one was open for 53% -> 0% of each run, Pallas kernels for 0% -> 0%
where the time goes in v1:
time: 81.4 us; the launch traced here: 81.3 us
  Pallas kernels  74.2 us (91%)
  local copies, waits for them, and re-layouts  6.37 us (8%)
    pallas_call x1, Pallas kernels, body(): pl.pallas_call(kernel, out_shape=(jax.ShapeDtypeStruct((ROWS, WIDTH), BF1...  74.2 us
    unnamed x14, local copies, waits for them, and re-layouts  6.37 us

profile of v1, /device:TPU:1, one launch (start us, length us, event | category | flops | bytes accessed | tf_op | source)
XLA Modules:
  0.0 81.3 jit_solution(18042309197690001668)
XLA Ops:
  0.6 74.2 %shard_map.136 = (bf16[128,1024]{1,0:T(8,128)(2,1)}, bf16[128,4096]{1,0:T(8,128)(2,1)}, f32[8,1024]{1,0:T(8,128)}, f32[1,1024]{1,0:T(1,128)}, f32[8,16]{1,0:T(8,128)}, /*index=5*/f32[8,16]{1,0:T(8,128)}) custom-call(bf16[128,4096]{1,0:T(8,128)(2,1)} %bitcast.7, bf16[128,1024]{1,0:T(8,128)(2,1)} %bitcast.9, s32[1,8]{1,0:T(1,128)} %lens.1, s32[1,128]{1,0:T(1,128)} %times.1, ...), custom_call_target="tpu_custom_call" | custom-call | tf_op jit(solution)/shard_map/pallas_call | solution.py:631
  74.9 0.0 copy-start
  74.9 0.0 copy-start.3
  74.9 0.0 copy-start.2
  74.9 0.0 copy-start.1
  74.9 1.7 %copy.21 = bf16[1,128,1024]{2,1,0:T(8,128)(2,1)} copy(bf16[1,128,1024]{2,1,0:T(8,128)(2,1)} %bitcast.11) | data formatting | bytes 524288
  76.6 2.3 %copy.22 = bf16[1,128,4096]{2,1,0:T(8,128)(2,1)} copy(bf16[1,128,4096]{2,1,0:T(8,128)(2,1)} %bitcast.8) | data formatting | bytes 2097152
  78.9 0.0 copy-done
  78.9 0.6 copy.23
  79.5 0.0 copy-done.3
  79.5 0.6 copy.24
  80.1 0.0 copy-done.2
  80.1 0.6 copy.25
  80.7 0.0 copy-done.1
  80.7 0.6 copy.26
Async XLA Ops:
  74.9 4.0 %copy-start = (f32[8,1024]{1,0:T(8,128)S(1)}, f32[8,1024]{1,0:T(8,128)}, u32[]{:S(2)}) copy-start(f32[8,1024]{1,0:T(8,128)} %get-tuple-element.26) | copy-start | bytes 98308
  74.9 4.6 %copy-start.3 = (f32[1,1024]{1,0:T(1,128)S(1)}, f32[1,1024]{1,0:T(1,128)}, u32[]{:S(2)}) copy-start(f32[1,1024]{1,0:T(1,128)} %get-tuple-element.15) | copy-start | bytes 12292
  74.9 5.2 %copy-start.2 = (f32[8,16]{1,0:T(8,128)S(1)}, f32[8,16]{1,0:T(8,128)}, u32[]{:S(2)}) copy-start(f32[8,16]{1,0:T(8,128)} %get-tuple-element.28) | copy-start | bytes 1540
  74.9 5.8 %copy-start.1 = (f32[8,16]{1,0:T(8,128)S(1)}, f32[8,16]{1,0:T(8,128)}, u32[]{:S(2)}) copy-start(f32[8,16]{1,0:T(8,128)} %get-tuple-element.29) | copy-start | bytes 1540

commit v2 on v1

--- a/solution.py
+++ b/solution.py
@@ -21,7 +21,7 @@
 FAR = 131072.0
 SCALE = ROWS ** (-0.5)
 
-KEY, VAL, TIM, QUE, DNO, END = 0, 128, 256, 272, 400, 528
+KEY, TIM, QUE, VAL, DNO, END = 0, 128, 144, 272, 400, 528
 CHUNKS = [(0, 256), (256, 256), (512, 256), (768, 256), (1024, 128)]
 
 NT = (((1,), (1,)), ((), ()))
@@ -54,14 +54,13 @@
 
 
 def kernel(
-    uvqk, resid, lens, times, ptab, ttab, gain, wout, cot,
-    out, dpre, dwo, dgain, dpos, dtime,
-    sb, rb, cot2, dh, kext, vall, aext, wa, pbias, wsave, fsave,
-    att_t, pn_t, gcol, att_s, att_r, stats, comb, dout, hid, hid_s, hid2,
-    ds_s, ds_r, e_s, e_r, diag, dkv, pacc, tmat, gacc, mq_s, mq_r, xs, xr, mk_s, mk_r,
-    tab, tab1, tab2,
-    loc_sem, m1s, m1r, m2s, m2r, fws, fwr, sib_s, sib_r, ats, atr, sts, str_,
-    d1s, d1r, d2s, d2r, qs, qr, ks, kr, t1s, t1r, t2s, t2r,
+    uvqk_h, resid_h, lens, times, ptab, ttab, gain, wout_h, cot_h,
+    out, dpu, mq_r, mk_r, dwo, dgain, dpos, dtime,
+    uvqk, resid, wout, cot8, sb, rb, dh, kext, vall, wa, pbias, wsave, fsave,
+    att_t, pn_t, gcol, att_s, att_r, stats, comb, dout, hid, hid_s, hid8,
+    e_s, e_r, diag, dkv, pacc, tmat, gacc, mq_s, xs, xr, mk_s, tab1, tab2,
+    loc_sem, m1s, m1r, m2s, m2r, m3s, m3r, fws, fwr, fvs, fvr, sib_s, sib_r, ats, atr, sts, str_,
+    cys, cyr, cfs, cfr, hs, hr, d2s, d2r, qs, qr, ks, kr, t1s, t1r, t2s, t2r,
 ):
     dp = lax.axis_index("dp")
     me = lax.axis_index("ctx")
@@ -70,6 +69,7 @@
     y = dp // 2
     zl = dp % 2
     sib = 2 * c + (1 - r)
+    spot = 2 * y + r
 
     def remote(src, dst, ssem, rsem, to):
         return pltpu.make_async_remote_copy(
@@ -77,6 +77,15 @@
             device_id_type=MESH,
         )
 
+    load_uvqk = pltpu.make_async_copy(uvqk_h, uvqk, loc_sem.at[0])
+    load_cot = pltpu.make_async_copy(cot_h, cot8.at[spot], loc_sem.at[1])
+    load_wout = pltpu.make_async_copy(wout_h, wout, loc_sem.at[2])
+    load_resid = pltpu.make_async_copy(resid_h, resid, loc_sem.at[3])
+    load_uvqk.start()
+    load_cot.start()
+    load_wout.start()
+    load_resid.start()
+
     barrier = pltpu.get_barrier_semaphore()
 
     def greet(j, _):
@@ -100,19 +109,23 @@
     time_rows = jnp.broadcast_to(times[...].astype(F32), (16, ROWS)).astype(BF16)
 
     def activate(h, _):
-        for group, where in ((3, KEY), (1, VAL), (2, QUE)):
+        for group, where in ((3, KEY), (2, QUE), (1, VAL)):
             x = 0.5 * uvqk[:, columns(group * HEADS + h)].astype(F32)
             sb[h, pl.ds(where, ROWS), :] = silu_half(x).astype(BF16)
         sb[h, pl.ds(TIM, 16), :] = time_rows
         return 0
 
+    load_uvqk.wait()
     lax.fori_loop(0, HEADS, activate, 0)
     pl.semaphore_wait(barrier, 37)
+
+    def block_rows(block):
+        return pl.ds(pl.multiple_of((block + PAD) * ROWS, ROWS), ROWS)
 
     def m1(k):
         to = (c + k) % CHIPS
         return remote(
-            sb.at[to, pl.ds(0, DNO)], rb.at[me, pl.ds(0, DNO)], m1s.at[k], m1r.at[k],
+            sb.at[to, pl.ds(0, VAL)], rb.at[me, pl.ds(0, VAL)], m1s.at[k], m1r.at[k],
             (dp, 2 * to + r),
         )
 
@@ -123,8 +136,18 @@
             (dp, 2 * to + r),
         )
 
+    def m3(k):
+        to = (c + k) % CHIPS
+        return remote(
+            sb.at[to, pl.ds(VAL, ROWS)], vall.at[block_rows(me)], m3s.at[k], m3r.at[k],
+            (dp, 2 * to + r),
+        )
+
     own_fw = remote(
         sb.at[c, pl.ds(0, QUE)], rb.at[me, pl.ds(0, QUE)], fws.at[0], fwr.at[0], (dp, sib)
+    )
+    own_fv = remote(
+        sb.at[c, pl.ds(VAL, ROWS)], vall.at[block_rows(me)], fvs.at[0], fvr.at[0], (dp, sib)
     )
 
     def fw(k):
@@ -134,18 +157,34 @@
             (dp, sib),
         )
 
-    cot_copy = remote(cot, cot2.at[pl.ds(ROWS, ROWS)], sib_s.at[0], sib_r.at[0], (dp, sib))
+    def fv(k):
+        at = block_rows(2 * ((c + CHIPS - k) % CHIPS) + r)
+        return remote(vall.at[at], vall.at[at], fvs.at[k], fvr.at[k], (dp, sib))
+
+    def cy(k):
+        return remote(
+            cot8.at[spot], cot8.at[spot], cys.at[k], cyr.at[k], (2 * ((y + k) % 4) + zl, me)
+        )
+
+    def cf(k):
+        at = 2 * ((y + 4 - k) % 4) + r
+        return remote(cot8.at[at], cot8.at[at], cfs.at[k], cfr.at[k], (dp, sib))
 
     for k in range(1, CHIPS):
         m1(k).start()
     own_fw.start()
-    cot_copy.start()
-    own1 = pltpu.make_async_copy(
-        sb.at[c, pl.ds(0, DNO)], rb.at[me, pl.ds(0, DNO)], loc_sem.at[0]
-    )
-    own1.start()
-
-    dh[...] = dot(cot[...], wout[...], NT)
+    for k in range(1, CHIPS):
+        m3(k).start()
+    own_fv.start()
+    rb[me, pl.ds(0, VAL), :] = sb[c, pl.ds(0, VAL), :]
+    vall[block_rows(me), :] = sb[c, pl.ds(VAL, ROWS), :]
+    load_cot.wait()
+    for k in range(1, 4):
+        cy(k).start()
+    cf(0).start()
+
+    load_wout.wait()
+    dh[...] = dot(cot8[spot], wout[...], NT)
 
     def d_normed(h, _):
         x = 0.5 * uvqk[:, columns(h)].astype(F32)
@@ -156,12 +195,8 @@
     lax.fori_loop(0, HEADS, d_normed, 0)
     for k in range(1, CHIPS):
         m2(k).start()
-    own2 = pltpu.make_async_copy(
-        sb.at[c, pl.ds(DNO, ROWS)], rb.at[me, pl.ds(DNO, ROWS)], loc_sem.at[1]
-    )
-    own2.start()
-
-    cot2[pl.ds(0, ROWS), :] = cot[...]
+    rb[me, pl.ds(DNO, ROWS), :] = sb[c, pl.ds(DNO, ROWS), :]
+
     kext[pl.ds(0, PAD * ROWS), :] = jnp.zeros((PAD * ROWS, 2 * ROWS), BF16)
     vall[pl.ds(0, PAD * ROWS), :] = jnp.zeros((PAD * ROWS, ROWS), BF16)
     dkv[...] = jnp.zeros_like(dkv)
@@ -206,7 +241,6 @@
     for k in range(1, CHIPS):
         m1(k).wait_recv()
         fw(k).start()
-    own1.wait()
     own_fw.wait_recv()
     for k in range(1, CHIPS):
         fw(k).wait_recv()
@@ -224,17 +258,12 @@
         index = jnp.where(sub < 48, sub % BUCKETS, sub - 48)
         value = jnp.where(sub < 48, t.astype(jnp.int32), jnp.where(sub < 56, user, -1))
         hot = jnp.where(index == value, 1.0, 0.0)
-        at = pl.ds(pl.multiple_of((block + PAD) * ROWS, ROWS), ROWS)
+        at = block_rows(block)
         kext[at, pl.ds(ROWS, ROWS)] = jnp.transpose(hot).astype(BF16)
         kext[at, pl.ds(0, ROWS)] = rb[block, pl.ds(KEY, ROWS), :]
-        vall[at, :] = rb[block, pl.ds(VAL, ROWS), :]
         return 0
 
     lax.fori_loop(0, 2 * CHIPS, features, 0)
-
-    for k in range(1, CHIPS):
-        m2(k).wait_recv()
-    own2.wait()
 
     def att_copy(k):
         t = (c + k) % CHIPS
@@ -243,13 +272,11 @@
     def window(b, first, size):
         return pl.ds(pl.multiple_of(b * ROWS + first, ROWS), size)
 
-    def forward(k, _):
+    def score(k, _):
         t = (c + k) % CHIPS
         b = 2 * t + r
-        own = pl.ds(pl.multiple_of((b + PAD) * ROWS, ROWS), ROWS)
-        feat = dot(kext[own, pl.ds(ROWS, ROWS)], wa[...]).astype(BF16)
+        feat = dot(kext[block_rows(b), pl.ds(ROWS, ROWS)], wa[...]).astype(BF16)
         query = jnp.concatenate([rb[b, pl.ds(QUE, ROWS), :], feat], axis=1)
-        total = jnp.zeros((ROWS, ROWS), F32)
         for first, size in CHUNKS:
             x = dot(query, kext[window(b, first, size), :], NT) * (0.5 * SCALE)
             x = x + pbias[:, pl.ds(first, size)]
@@ -257,9 +284,24 @@
             a = 1.0 + th
             w = x * a
             fsave[t, :, pl.ds(first, size)] = a + w * (1.0 - th)
-            w = w.astype(BF16)
-            wsave[t, :, pl.ds(first, size)] = w
-            total = total + dot(w, vall[window(b, first, size), :])
+            wsave[t, :, pl.ds(first, size)] = w.astype(BF16)
+        return 0
+
+    lax.fori_loop(0, 5, score, 0)
+    for k in range(1, CHIPS):
+        m3(k).wait_recv()
+        fv(k).start()
+    lax.fori_loop(5, CHIPS, score, 0)
+    own_fv.wait_recv()
+    for k in range(1, CHIPS):
+        fv(k).wait_recv()
+    for k in range(1, CHIPS):
+        m2(k).wait_recv()
+
+    def attend(k, _):
+        t = (c + k) % CHIPS
+        b = 2 * t + r
+        total = dot(wsave[t], vall[window(b, 0, WIN), :])
         att_s[t] = total.astype(BF16)
 
         @pl.when(k > 0)
@@ -280,7 +322,7 @@
         stats[c, 3, row, :] = jnp.sum(g, axis=0, keepdims=True)
         return 0
 
-    lax.fori_loop(0, CHIPS, forward, 0)
+    lax.fori_loop(0, CHIPS, attend, 0)
 
     def stat_copy(k):
         to = (c + k) % CHIPS
@@ -295,6 +337,9 @@
     for k in range(1, CHIPS):
         stat_copy(k).start()
     att_r[c] = att_s[c]
+    for k in range(1, 4):
+        cy(k).wait_recv()
+        cf(k).start()
     for k in range(1, CHIPS):
         stat_recv(k).wait_recv()
 
@@ -342,30 +387,24 @@
         s = x * a
         hidden = (normed * s.astype(BF16).astype(F32)).astype(BF16)
         hid[:, columns(h)] = hidden
-        hid_s[h % 2, h // 2] = hidden
+        hid_s[h] = hidden
         d_u = dh[:, columns(h)] * normed
-        dpre[:, columns(h)] = (d_u * (0.5 * (a + s * (1.0 - t)))).astype(BF16)
+        dpu[:, columns(h)] = (d_u * (0.5 * (a + s * (1.0 - t)))).astype(BF16)
         return 0
 
     lax.fori_loop(0, HEADS, rows_of, 0)
-    hid_copy = remote(
-        hid_s.at[1 - r], hid2.at[:, pl.ds(ROWS, ROWS), :], sib_s.at[1], sib_r.at[1], (dp, sib)
-    )
-    hid_copy.start()
-    hid2[:, pl.ds(0, ROWS), :] = hid_s[r]
-    out[...] = (resid[...].astype(F32) + dot(hid[...], wout[...])).astype(BF16)
-    cot_copy.wait_recv()
-    hid_copy.wait_recv()
-
-    def d1(k):
-        to = (y + k) % 4
-        return remote(ds_s.at[to], ds_r.at[y], d1s.at[k], d1r.at[k], (2 * to + zl, me))
-
-    for k in range(1, 5):
-        to = (y + k) % 4
-        ds_s[to] = dot(hid2[to], cot2[...], TN).astype(BF16)
-        if k < 4:
-            d1(k).start()
+
+    def hid_to(j):
+        y_to = (y + j // 2) % 4
+        r_to = (r + j) % 2
+        return remote(
+            hid_s.at[2 * y_to + r_to], hid8.at[spot], hs.at[j], hr.at[j],
+            (2 * y_to + zl, 2 * c + r_to),
+        )
+
+    for j in range(1, 8):
+        hid_to(j).start()
+    hid8[spot] = hid_s[spot]
 
     def dq_copy(k):
         t = (c + k) % CHIPS
@@ -395,12 +434,48 @@
 
         high = dq[:, ROWS:].astype(BF16)
         low = (dq[:, ROWS:] - high.astype(F32)).astype(BF16)
-        own = pl.ds(pl.multiple_of((b + PAD) * ROWS, ROWS), ROWS)
-        hot = kext[own, pl.ds(ROWS, ROWS)]
+        hot = kext[block_rows(b), pl.ds(ROWS, ROWS)]
         tmat[...] += dot(hot, high, TN) + dot(hot, low, TN)
         return 0
 
-    lax.fori_loop(0, CHIPS, backward, 0)
+    lax.fori_loop(0, 4, backward, 0)
+
+    for j in range(1, 8):
+        hid_to(j).wait_recv()
+    for k in range(4):
+        cf(k).wait_recv()
+    left = hid8[...].reshape(8 * ROWS, ROWS)
+    for first in range(0, WIDTH, 256):
+        some = pl.ds(first, 256)
+        total = dot(left, cot8[:, :, some].reshape(8 * ROWS, 256), TN)
+        e_s[:, :, some] = total.reshape(16, 8, 256)
+
+    slot = zl * CHIPS + c
+
+    def d2(j):
+        to = (me + j) % 16
+        return remote(e_s.at[to], e_r.at[slot], d2s.at[j], d2r.at[slot], (2 * y + r, to))
+
+    def d2_recv(j):
+        z_from = (zl + j // CHIPS) % 2
+        c_from = (c + j % CHIPS) % CHIPS
+        here = z_from * CHIPS + c_from
+        return remote(
+            e_s.at[0], e_r.at[here], d2s.at[0], d2r.at[here], (2 * y + z_from, 2 * c_from + zl)
+        )
+
+    for j in range(1, 16):
+        d2(j).start()
+
+    @pl.when(r != zl)
+    def _():
+        d2(0).start()
+
+    @pl.when(r == zl)
+    def _():
+        e_r[slot] = e_s[me]
+
+    lax.fori_loop(4, CHIPS, backward, 0)
 
     def to_sibling(t, _):
         at = pl.ds(pl.multiple_of((2 * t + (1 - r) + PAD) * ROWS, ROWS), ROWS)
@@ -408,7 +483,7 @@
         return 0
 
     lax.fori_loop(0, CHIPS, to_sibling, 0)
-    dkv_copy = remote(xs, xr, sib_s.at[2], sib_r.at[2], (dp, sib))
+    dkv_copy = remote(xs, xr, sib_s.at[0], sib_r.at[0], (dp, sib))
     dkv_copy.start()
 
     sums = []
@@ -465,42 +540,8 @@
     lax.fori_loop(0, CHIPS, join, 0)
     mq_r[c] = mq_s[c]
     mk_r[c] = mk_s[c]
-
-    for k in range(1, 4):
-        d1(k).wait_recv()
-    ds_r[y] = ds_s[y]
-    for pair in range(CHIPS):
-        at = pl.ds(pair * 16, 16)
-        total = ds_r[0, at, :].astype(F32)
-        for k in range(1, 4):
-            total = total + ds_r[k, at, :].astype(F32)
-        e_s[2 * pair] = total[:8]
-        e_s[2 * pair + 1] = total[8:]
-
-    slot = zl * CHIPS + c
-
-    def d2(j):
-        to = (me + j) % 16
-        return remote(e_s.at[to], e_r.at[slot], d2s.at[j], d2r.at[slot], (2 * y + r, to))
-
-    def d2_recv(j):
-        z_from = (zl + j // CHIPS) % 2
-        c_from = (c + j % CHIPS) % CHIPS
-        here = z_from * CHIPS + c_from
-        return remote(
-            e_s.at[0], e_r.at[here], d2s.at[0], d2r.at[here], (2 * y + z_from, 2 * c_from + zl)
-        )
-
-    for j in range(1, 16):
-        d2(j).start()
-
-    @pl.when(r != zl)
-    def _():
-        d2(0).start()
-
-    @pl.when(r == zl)
-    def _():
-        e_r[slot] = e_s[me]
+    load_resid.wait()
+    out[...] = (resid[...].astype(F32) + dot(hid[...], wout[...])).astype(BF16)
 
     for k in range(1, 8):
         t1_recv(k).wait_recv()
@@ -518,20 +559,6 @@
 
     for k in range(1, 16):
         t2(k).start()
-
-    for k in range(1, CHIPS):
-        dq_copy(k).wait_recv()
-    for k in range(1, CHIPS):
-        kv_copy(k).wait_recv()
-
-    def finish(h, _):
-        for group, value in ((1, mk_r[h, 1]), (2, mq_r[h]), (3, mk_r[h, 0])):
-            at = columns(group * HEADS + h)
-            x = 0.5 * uvqk[:, at].astype(F32)
-            dpre[:, at] = (value.astype(F32) * silu_grad_half(x)).astype(BF16)
-        return 0
-
-    lax.fori_loop(0, HEADS, finish, 0)
 
     for k in range(1, 16):
         t2_recv(k).wait_recv()
@@ -554,24 +581,48 @@
         total = total + e_r[k]
     dwo[...] = total
 
+    for k in range(1, CHIPS):
+        dq_copy(k).wait_recv()
+    for k in range(1, CHIPS):
+        kv_copy(k).wait_recv()
+
     own_fw.wait_send()
-    cot_copy.wait_send()
-    hid_copy.wait_send()
+    own_fv.wait_send()
     dkv_copy.wait_send()
+    for k in range(4):
+        cf(k).wait_send()
     for k in range(1, CHIPS):
         m1(k).wait_send()
         m2(k).wait_send()
+        m3(k).wait_send()
         fw(k).wait_send()
+        fv(k).wait_send()
+        hid_to(k).wait_send()
         att_copy(k).wait_send()
         stat_copy(k).wait_send()
         dq_copy(k).wait_send()
         kv_copy(k).wait_send()
         t1(k).wait_send()
     for k in range(1, 4):
-        d1(k).wait_send()
+        cy(k).wait_send()
     for k in range(1, 16):
         d2(k).wait_send()
         t2(k).wait_send()
+
+
+def finish(uvqk, out_k, dpu, dq, dkv, dwo_k, dgain_k, dpos_k, dtime_k,
+           out, dpre, dwo, dgain, dpos, dtime):
+    out[...] = out_k[...]
+    dpre[:, pl.ds(0, WIDTH)] = dpu[...]
+    for h in range(HEADS):
+        for group, value in ((1, dkv[h, 1]), (2, dq[h]), (3, dkv[h, 0])):
+            at = pl.ds((group * HEADS + h) * ROWS, ROWS)
+            x = 0.5 * uvqk[:, at].astype(F32)
+            dpre[:, at] = (value.astype(F32) * silu_grad_half(x)).astype(BF16)
+    dwo[...] = dwo_k[...]
+    dgain[...] = dgain_k[...]
+    dpos[...] = dpos_k[...]
+    dtime[...] = dtime_k[...]
 
 
 def body(
@@ -579,17 +630,20 @@
 ):
     vm = pl.BlockSpec(memory_space=pltpu.VMEM)
     sm = pl.BlockSpec(memory_space=pltpu.SMEM)
+    hbm = pl.BlockSpec(memory_space=pl.ANY)
     tile = (ROWS, ROWS)
     dma = pltpu.SemaphoreType.DMA
     padded = (2 * CHIPS + PAD) * ROWS
     scratch = [
+        pltpu.VMEM((ROWS, 4 * WIDTH), BF16),
+        pltpu.VMEM((ROWS, WIDTH), BF16),
+        pltpu.VMEM((WIDTH, WIDTH), BF16),
+        pltpu.VMEM((8, ROWS, WIDTH), BF16),
         pltpu.VMEM((HEADS, END, ROWS), BF16),
         pltpu.VMEM((2 * CHIPS, END, ROWS), BF16),
-        pltpu.VMEM((2 * ROWS, WIDTH), BF16),
         pltpu.VMEM((ROWS, WIDTH), F32),
         pltpu.VMEM((padded, 2 * ROWS), BF16),
         pltpu.VMEM((padded, ROWS), BF16),
-        pltpu.VMEM(tile, BF16),
         pltpu.VMEM(tile, BF16),
         pltpu.VMEM((ROWS, WIN), F32),
         pltpu.VMEM((CHIPS, ROWS, WIN), BF16),
@@ -603,10 +657,8 @@
         pltpu.VMEM((4, CHIPS, ROWS), F32),
         pltpu.VMEM((CHIPS,) + tile, BF16),
         pltpu.VMEM((ROWS, WIDTH), BF16),
-        pltpu.VMEM((2, 4) + tile, BF16),
-        pltpu.VMEM((4, 2 * ROWS, ROWS), BF16),
-        pltpu.VMEM((4, ROWS, WIDTH), BF16),
-        pltpu.VMEM((4, ROWS, WIDTH), BF16),
+        pltpu.VMEM((8,) + tile, BF16),
+        pltpu.VMEM((8,) + tile, BF16),
         pltpu.VMEM((16, 8, WIDTH), F32),
         pltpu.VMEM((16, 8, WIDTH), F32),
         pltpu.VMEM((2 * ROWS, 2 * ROWS), BF16),
@@ -615,21 +667,53 @@
         pltpu.VMEM(tile, F32),
         pltpu.VMEM(tile, F32),
         pltpu.VMEM((CHIPS,) + tile, BF16),
-        pltpu.VMEM((HEADS,) + tile, BF16),
         pltpu.VMEM((CHIPS, ROWS, 2 * ROWS), BF16),
         pltpu.VMEM((CHIPS, ROWS, 2 * ROWS), BF16),
         pltpu.VMEM((CHIPS, 2) + tile, BF16),
-        pltpu.VMEM((HEADS, 2) + tile, BF16),
-        pltpu.VMEM((8, ROWS), F32),
         pltpu.VMEM((8, 8, ROWS), F32),
         pltpu.VMEM((16, 8, ROWS), F32),
-        dma((2,)),
+        dma((4,)),
     ] + [
         dma((count,))
-        for count in (8, 8, 8, 8, 8, 8, 3, 3, 8, 8, 8, 8, 4, 4, 16, 16, 8, 8, 8, 8, 8, 8, 16, 16)
+        for count in (
+            8, 8, 8, 8, 8, 8, 8, 8, 8, 8, 1, 1, 8, 8, 8, 8,
+            4, 4, 4, 4, 8, 8, 16, 16, 8, 8, 8, 8, 8, 8, 16, 16,
+        )
     ]
+    partial = pl.pallas_call(
+        kernel,
+        out_shape=(
+            jax.ShapeDtypeStruct((ROWS, WIDTH), BF16),
+            jax.ShapeDtypeStruct((ROWS, WIDTH), BF16),
+            jax.ShapeDtypeStruct((HEADS,) + tile, BF16),
+            jax.ShapeDtypeStruct((HEADS, 2) + tile, BF16),
+            jax.ShapeDtypeStruct((8, WIDTH), F32),
+            jax.ShapeDtypeStruct((1, WIDTH), F32),
+            jax.ShapeDtypeStruct((HEADS, BUCKETS), F32),
+            jax.ShapeDtypeStruct((HEADS, BUCKETS), F32),
+        ),
+        in_specs=[hbm, hbm, sm, vm, sm, sm, vm, hbm, hbm],
+        out_specs=(vm,) * 8,
+        scratch_shapes=scratch,
+        compiler_params=pltpu.CompilerParams(
+            collective_id=0, has_side_effects=True, vmem_limit_bytes=63 * 1024 * 1024
+        ),
+    )(
+        uvqk[0], residual[0], lengths, time_buckets, pos_table, time_table,
+        output_norm_gain[None], w_out, cotangent[0],
+    )
+    steps = 4
+    some = ROWS // steps
+
+    def whole(*shape):
+        return pl.BlockSpec(shape, lambda i: (0,) * len(shape))
+
+    wide = pl.BlockSpec((some, 4 * WIDTH), lambda i: (i, 0))
+    narrow = pl.BlockSpec((some, WIDTH), lambda i: (i, 0))
+    small = [whole(8, WIDTH), whole(1, WIDTH), whole(HEADS, BUCKETS), whole(HEADS, BUCKETS)]
     out, dpre, dwo, dgain, dpos, dtime = pl.pallas_call(
-        kernel,
+        finish,
+        grid=(steps,),
         out_shape=(
             jax.ShapeDtypeStruct((ROWS, WIDTH), BF16),
             jax.ShapeDtypeStruct((ROWS, 4 * WIDTH), BF16),
@@ -638,16 +722,14 @@
             jax.ShapeDtypeStruct((HEADS, BUCKETS), F32),
             jax.ShapeDtypeStruct((HEADS, BUCKETS), F32),
         ),
-        in_specs=[vm, vm, sm, vm, sm, sm, vm, vm, vm],
-        out_specs=(vm,) * 6,
-        scratch_shapes=scratch,
-        compiler_params=pltpu.CompilerParams(
-            collective_id=0, has_side_effects=True, vmem_limit_bytes=56 * 1024 * 1024
-        ),
-    )(
-        uvqk[0], residual[0], lengths, time_buckets, pos_table, time_table,
-        output_norm_gain[None], w_out, cotangent[0],
-    )
+        in_specs=[
+            wide, narrow, narrow,
+            pl.BlockSpec((HEADS, some, ROWS), lambda i: (0, i, 0)),
+            pl.BlockSpec((HEADS, 2, some, ROWS), lambda i: (0, 0, i, 0)),
+        ] + small,
+        out_specs=[narrow, wide] + small,
+        compiler_params=pltpu.CompilerParams(vmem_limit_bytes=63 * 1024 * 1024),
+    )(uvqk[0], *partial)
     return (out[None], dpre[None], dwo, dgain[0], dpos, dtime)
 
 

time: 81.4 us -> 70.4 us (0.86)
  local copies, waits for them, and re-layouts: 6.37 us -> 0 us
  Pallas kernels: 74.2 us -> 69.5 us
    pallas_call x1, Pallas kernels: 74.2 us -> 65.6 us  [body(): pl.pallas_call(kernel, out_shape=(jax.ShapeDtypeStruct((ROWS, WIDTH), BF1...]
    unnamed x14 -> x0, local copies, waits for them, and re-layouts: 6.37 us -> none
    pallas_call x0 -> x1, Pallas kernels: none -> 3.97 us  [body(): pl.pallas_call(finish, grid=(steps,), out_shape=(jax.ShapeDtypeStruct((RO...]
where the time goes in v2:
time: 70.4 us; the launch traced here: 70.2 us
  Pallas kernels  69.5 us (99%)
    pallas_call x1, Pallas kernels, body(): pl.pallas_call(kernel, out_shape=(jax.ShapeDtypeStruct((ROWS, WIDTH), BF1...  65.6 us
    pallas_call x1, Pallas kernels, body(): pl.pallas_call(finish, grid=(steps,), out_shape=(jax.ShapeDtypeStruct((RO...  3.97 us

profile of v2, /device:TPU:1, one launch (start us, length us, event | category | flops | bytes accessed | tf_op | source)
XLA Modules:
  0.0 70.2 jit_solution(6417873045547718683)
XLA Ops:
  0.6 65.6 %shard_map.136 = (bf16[128,1024]{1,0:T(8,128)(2,1)}, bf16[128,1024]{1,0:T(8,128)(2,1)}, bf16[8,128,128]{2,1,0:T(8,128)(2,1)}, bf16[8,2,128,128]{3,2,1,0:T(8,128)...) custom-call(bf16[128,4096]{1,0:T(8,128)(2,1)} %bitcast.7, ...), custom_call_target="tpu_custom_call" | custom-call | tf_op jit(solution)/shard_map/pallas_call | solution.py:683
  66.2 4.0 %shard_map.137 = (bf16[128,1024]{1,0:T(8,128)(2,1)}, bf16[128,4096]{1,0:T(8,128)(2,1)}, f32[8,1024]{1,0:T(8,128)}, f32[1,1024]{1,0:T(1,128)}, f32[8,16]{1,0:T(8,128)}, /*index=5*/f32[8,16]{1,0:T(8,128)}) custom-call(bf16[128,4096]{1,0:T(8,128)(2,1)} %bitcast.8, bf16[128,1024]{1,0:T(8,128)(2,1)} %get-tuple-element.20.out_k, ...), custom_call_target="tpu_custom_call" | custom-call | tf_op jit(solution)/shard_map/pallas_call | solution.py:714

commit v3 on v2

--- a/solution.py
+++ b/solution.py
@@ -58,7 +58,7 @@
     out, dpu, mq_r, mk_r, dwo, dgain, dpos, dtime,
     uvqk, resid, wout, cot8, sb, rb, dh, kext, vall, wa, pbias, wsave, fsave,
     att_t, pn_t, gcol, att_s, att_r, stats, comb, dout, hid, hid_s, hid8,
-    e_s, e_r, diag, dkv, pacc, tmat, gacc, mq_s, xs, xr, mk_s, tab1, tab2,
+    e_s, e_r, diag, dq_t, dkv, pacc, tmat, gacc, mq_s, xs, xr, mk_s, tab1, tab2,
     loc_sem, m1s, m1r, m2s, m2r, m3s, m3r, fws, fwr, fvs, fvr, sib_s, sib_r, ats, atr, sts, str_,
     cys, cyr, cfs, cfr, hs, hr, d2s, d2r, qs, qr, ks, kr, t1s, t1r, t2s, t2r,
 ):
@@ -109,7 +109,7 @@
     time_rows = jnp.broadcast_to(times[...].astype(F32), (16, ROWS)).astype(BF16)
 
     def activate(h, _):
-        for group, where in ((3, KEY), (2, QUE), (1, VAL)):
+        for group, where in ((3, KEY), (2, QUE)):
             x = 0.5 * uvqk[:, columns(group * HEADS + h)].astype(F32)
             sb[h, pl.ds(where, ROWS), :] = silu_half(x).astype(BF16)
         sb[h, pl.ds(TIM, 16), :] = time_rows
@@ -173,9 +173,13 @@
     for k in range(1, CHIPS):
         m1(k).start()
     own_fw.start()
-    for k in range(1, CHIPS):
-        m3(k).start()
-    own_fv.start()
+
+    def activate_values(h, _):
+        x = 0.5 * uvqk[:, columns(HEADS + h)].astype(F32)
+        sb[h, pl.ds(VAL, ROWS), :] = silu_half(x).astype(BF16)
+        return 0
+
+    lax.fori_loop(0, HEADS, activate_values, 0)
     rb[me, pl.ds(0, VAL), :] = sb[c, pl.ds(0, VAL), :]
     vall[block_rows(me), :] = sb[c, pl.ds(VAL, ROWS), :]
     load_cot.wait()
@@ -193,8 +197,6 @@
         return 0
 
     lax.fori_loop(0, HEADS, d_normed, 0)
-    for k in range(1, CHIPS):
-        m2(k).start()
     rb[me, pl.ds(DNO, ROWS), :] = sb[c, pl.ds(DNO, ROWS), :]
 
     kext[pl.ds(0, PAD * ROWS), :] = jnp.zeros((PAD * ROWS, 2 * ROWS), BF16)
@@ -239,11 +241,18 @@
         pbias[:, pl.ds(w * ROWS, ROWS)] = tile
 
     for k in range(1, CHIPS):
+        m3(k).start()
+    own_fv.start()
+
+    for k in range(1, CHIPS):
         m1(k).wait_recv()
         fw(k).start()
     own_fw.wait_recv()
     for k in range(1, CHIPS):
         fw(k).wait_recv()
+
+    for k in range(1, CHIPS):
+        m2(k).start()
 
     ends = [lens[0, 0]]
     for k in range(1, 7):
@@ -272,19 +281,30 @@
     def window(b, first, size):
         return pl.ds(pl.multiple_of(b * ROWS + first, ROWS), size)
 
+    def for_reach(t, run):
+        for reach in (2, 4, 6, SPAN):
+            @pl.when((t == reach // 2 - 1) if reach < SPAN else (t >= 3))
+            def _():
+                run((SPAN - reach) * ROWS, reach * ROWS)
+
     def score(k, _):
         t = (c + k) % CHIPS
         b = 2 * t + r
         feat = dot(kext[block_rows(b), pl.ds(ROWS, ROWS)], wa[...]).astype(BF16)
         query = jnp.concatenate([rb[b, pl.ds(QUE, ROWS), :], feat], axis=1)
-        for first, size in CHUNKS:
-            x = dot(query, kext[window(b, first, size), :], NT) * (0.5 * SCALE)
-            x = x + pbias[:, pl.ds(first, size)]
-            th = jnp.tanh(x)
-            a = 1.0 + th
-            w = x * a
-            fsave[t, :, pl.ds(first, size)] = a + w * (1.0 - th)
-            wsave[t, :, pl.ds(first, size)] = w.astype(BF16)
+
+        def run(start, length):
+            for first in range(start, WIN, 256):
+                size = min(256, WIN - first)
+                x = dot(query, kext[window(b, first, size), :], NT) * (0.5 * SCALE)
+                x = x + pbias[:, pl.ds(first, size)]
+                th = jnp.tanh(x)
+                a = 1.0 + th
+                w = x * a
+                fsave[t, :, pl.ds(first, size)] = a + w * (1.0 - th)
+                wsave[t, :, pl.ds(first, size)] = w.astype(BF16)
+
+        for_reach(t, run)
         return 0
 
     lax.fori_loop(0, 5, score, 0)
@@ -295,34 +315,41 @@
     own_fv.wait_recv()
     for k in range(1, CHIPS):
         fv(k).wait_recv()
-    for k in range(1, CHIPS):
-        m2(k).wait_recv()
 
     def attend(k, _):
         t = (c + k) % CHIPS
-        b = 2 * t + r
-        total = dot(wsave[t], vall[window(b, 0, WIN), :])
-        att_s[t] = total.astype(BF16)
-
-        @pl.when(k > 0)
-        def _():
-            att_copy(k).start()
-
-        tr = jnp.transpose(total)
-        att_t[t] = tr
-        pn = jnp.transpose(rb[b, pl.ds(DNO, ROWS), :].astype(F32))
-        pn_t[t] = pn
-        g = pn * gcol[...]
+
+        def run(start, length):
+            total = dot(
+                wsave[t, :, pl.ds(start, length)], vall[window(2 * t + r, start, length), :]
+            )
+            att_s[t] = total.astype(BF16)
+            att_t[t] = jnp.transpose(total)
+
+        for_reach(t, run)
+        tr = att_t[t]
         mean = jnp.sum(tr, axis=0, keepdims=True) * (1.0 / ROWS)
         dev = tr - mean
         row = pl.ds(t, 1)
         stats[c, 0, row, :] = mean
         stats[c, 1, row, :] = jnp.sum(dev * dev, axis=0, keepdims=True)
+        return 0
+
+    lax.fori_loop(0, CHIPS, attend, 0)
+    for k in range(1, CHIPS):
+        m2(k).wait_recv()
+
+    def moments(t, _):
+        pn = jnp.transpose(rb[2 * t + r, pl.ds(DNO, ROWS), :].astype(F32))
+        pn_t[t] = pn
+        g = pn * gcol[...]
+        row = pl.ds(t, 1)
+        dev = att_t[t] - stats[c, 0, row, :]
         stats[c, 2, row, :] = jnp.sum(dev * g, axis=0, keepdims=True)
         stats[c, 3, row, :] = jnp.sum(g, axis=0, keepdims=True)
         return 0
 
-    lax.fori_loop(0, CHIPS, attend, 0)
+    lax.fori_loop(0, CHIPS, moments, 0)
 
     def stat_copy(k):
         to = (c + k) % CHIPS
@@ -336,6 +363,8 @@
 
     for k in range(1, CHIPS):
         stat_copy(k).start()
+    for k in range(1, CHIPS):
+        att_copy(k).start()
     att_r[c] = att_s[c]
     for k in range(1, 4):
         cy(k).wait_recv()
@@ -373,6 +402,43 @@
 
     lax.fori_loop(0, CHIPS, d_attended, 0)
 
+    def dq_copy(k):
+        t = (c + k) % CHIPS
+        return remote(mq_s.at[t], mq_r.at[c], qs.at[k], qr.at[k], (dp, 2 * t + r))
+
+    def backward(k, _):
+        t = (c + k) % CHIPS
+        b = 2 * t + r
+        d = dout[t]
+        diag[pl.ds(0, ROWS), pl.ds(0, ROWS)] = rb[b, pl.ds(QUE, ROWS), :]
+        diag[pl.ds(ROWS, ROWS), pl.ds(ROWS, ROWS)] = d
+        both = diag[...]
+
+        def run(start, length):
+            at = window(b, start, length)
+            some = pl.ds(start, length)
+            ds = dot(d, vall[at, :], NT) * fsave[t, :, some]
+            pacc[:, some] += ds
+            ds = ds.astype(BF16)
+            dq_t[...] = dot(ds, kext[at, :])
+            dkv[at, :] += dot(jnp.concatenate([ds, wsave[t, :, some]], axis=0), both, TN)
+
+        for_reach(t, run)
+        dq = dq_t[...]
+        mq_s[t] = (dq[:, :ROWS] * SCALE).astype(BF16)
+
+        @pl.when(k > 0)
+        def _():
+            dq_copy(k).start()
+
+        high = dq[:, ROWS:].astype(BF16)
+        low = (dq[:, ROWS:] - high.astype(F32)).astype(BF16)
+        hot = kext[block_rows(b), pl.ds(ROWS, ROWS)]
+        tmat[...] += dot(hot, high, TN) + dot(hot, low, TN)
+        return 0
+
+    lax.fori_loop(0, 2, backward, 0)
+
     mine = pl.ds(c, 1)
     mean_c = jnp.transpose(jnp.broadcast_to(comb[0, mine, :], (ROWS, ROWS)))
     inv_c = jnp.transpose(jnp.broadcast_to(comb[1, mine, :], (ROWS, ROWS)))
@@ -406,76 +472,7 @@
         hid_to(j).start()
     hid8[spot] = hid_s[spot]
 
-    def dq_copy(k):
-        t = (c + k) % CHIPS
-        return remote(mq_s.at[t], mq_r.at[c], qs.at[k], qr.at[k], (dp, 2 * t + r))
-
-    def backward(k, _):
-        t = (c + k) % CHIPS
-        b = 2 * t + r
-        d = dout[t]
-        diag[pl.ds(0, ROWS), pl.ds(0, ROWS)] = rb[b, pl.ds(QUE, ROWS), :]
-        diag[pl.ds(ROWS, ROWS), pl.ds(ROWS, ROWS)] = d
-        both = diag[...]
-        dq = jnp.zeros((ROWS, 2 * ROWS), F32)
-        for first, size in CHUNKS:
-            at = window(b, first, size)
-            some = pl.ds(first, size)
-            ds = dot(d, vall[at, :], NT) * fsave[t, :, some]
-            pacc[:, some] += ds
-            ds = ds.astype(BF16)
-            dq = dq + dot(ds, kext[at, :])
-            dkv[at, :] += dot(jnp.concatenate([ds, wsave[t, :, some]], axis=0), both, TN)
-        mq_s[t] = (dq[:, :ROWS] * SCALE).astype(BF16)
-
-        @pl.when(k > 0)
-        def _():
-            dq_copy(k).start()
-
-        high = dq[:, ROWS:].astype(BF16)
-        low = (dq[:, ROWS:] - high.astype(F32)).astype(BF16)
-        hot = kext[block_rows(b), pl.ds(ROWS, ROWS)]
-        tmat[...] += dot(hot, high, TN) + dot(hot, low, TN)
-        return 0
-
-    lax.fori_loop(0, 4, backward, 0)
-
-    for j in range(1, 8):
-        hid_to(j).wait_recv()
-    for k in range(4):
-        cf(k).wait_recv()
-    left = hid8[...].reshape(8 * ROWS, ROWS)
-    for first in range(0, WIDTH, 256):
-        some = pl.ds(first, 256)
-        total = dot(left, cot8[:, :, some].reshape(8 * ROWS, 256), TN)
-        e_s[:, :, some] = total.reshape(16, 8, 256)
-
-    slot = zl * CHIPS + c
-
-    def d2(j):
-        to = (me + j) % 16
-        return remote(e_s.at[to], e_r.at[slot], d2s.at[j], d2r.at[slot], (2 * y + r, to))
-
-    def d2_recv(j):
-        z_from = (zl + j // CHIPS) % 2
-        c_from = (c + j % CHIPS) % CHIPS
-        here = z_from * CHIPS + c_from
-        return remote(
-            e_s.at[0], e_r.at[here], d2s.at[0], d2r.at[here], (2 * y + z_from, 2 * c_from + zl)
-        )
-
-    for j in range(1, 16):
-        d2(j).start()
-
-    @pl.when(r != zl)
-    def _():
-        d2(0).start()
-
-    @pl.when(r == zl)
-    def _():
-        e_r[slot] = e_s[me]
-
-    lax.fori_loop(4, CHIPS, backward, 0)
+    lax.fori_loop(2, CHIPS, backward, 0)
 
     def to_sibling(t, _):
         at = pl.ds(pl.multiple_of((2 * t + (1 - r) + PAD) * ROWS, ROWS), ROWS)
@@ -518,6 +515,60 @@
     for k in range(1, 8):
         t1(k).start()
 
+    for j in range(1, 8):
+        hid_to(j).wait_recv()
+    for k in range(4):
+        cf(k).wait_recv()
+    left = hid8[...].reshape(8 * ROWS, ROWS)
+    for first in range(0, WIDTH // 2, 256):
+        parts = [
+            dot(left, cot8[:, :, pl.ds(at, 256)].reshape(8 * ROWS, 256), TN).reshape(16, 8, 256)
+            for at in (first, first + WIDTH // 2)
+        ]
+        e_s[:, :, pl.ds(first, 256)] = jnp.concatenate(parts, axis=1).astype(BF16)
+
+    slot = zl * CHIPS + c
+
+    def d2(j):
+        to = (me + j) % 16
+        return remote(e_s.at[to], e_r.at[slot], d2s.at[j], d2r.at[slot], (2 * y + r, to))
+
+    def d2_recv(j):
+        z_from = (zl + j // CHIPS) % 2
+        c_from = (c + j % CHIPS) % CHIPS
+        here = z_from * CHIPS + c_from
+        return remote(
+            e_s.at[0], e_r.at[here], d2s.at[0], d2r.at[here], (2 * y + z_from, 2 * c_from + zl)
+        )
+
+    for j in range(1, 16):
+        d2(j).start()
+
+    @pl.when(r != zl)
+    def _():
+        d2(0).start()
+
+    @pl.when(r == zl)
+    def _():
+        e_r[slot] = e_s[me]
+
+    for k in range(1, 8):
+        t1_recv(k).wait_recv()
+    total = tab1[0]
+    for k in range(1, 8):
+        total = total + tab1[k]
+    tab2[me] = total
+
+    def t2(k):
+        return remote(tab2.at[me], tab2.at[me], t2s.at[k], t2r.at[k], (dp, (me + k) % 16))
+
+    def t2_recv(k):
+        source = (me + 16 - k) % 16
+        return remote(tab2.at[source], tab2.at[source], t2s.at[k], t2r.at[k], (dp, source))
+
+    for k in range(1, 16):
+        t2(k).start()
+
     dkv_copy.wait_recv()
 
     def kv_copy(k):
@@ -543,22 +594,6 @@
     load_resid.wait()
     out[...] = (resid[...].astype(F32) + dot(hid[...], wout[...])).astype(BF16)
 
-    for k in range(1, 8):
-        t1_recv(k).wait_recv()
-    total = tab1[0]
-    for k in range(1, 8):
-        total = total + tab1[k]
-    tab2[me] = total
-
-    def t2(k):
-        return remote(tab2.at[me], tab2.at[me], t2s.at[k], t2r.at[k], (dp, (me + k) % 16))
-
-    def t2_recv(k):
-        source = (me + 16 - k) % 16
-        return remote(tab2.at[source], tab2.at[source], t2s.at[k], t2r.at[k], (dp, source))
-
-    for k in range(1, 16):
-        t2(k).start()
 
     for k in range(1, 16):
         t2_recv(k).wait_recv()
@@ -576,10 +611,11 @@
         d2_recv(0).wait_recv()
         d2(0).wait_send()
 
-    total = e_r[0]
+    total = e_r[0].astype(F32)
     for k in range(1, 16):
-        total = total + e_r[k]
-    dwo[...] = total
+        total = total + e_r[k].astype(F32)
+    dwo[:, pl.ds(0, WIDTH // 2)] = total[:8]
+    dwo[:, pl.ds(WIDTH // 2, WIDTH // 2)] = total[8:]
 
     for k in range(1, CHIPS):
         dq_copy(k).wait_recv()
@@ -659,9 +695,10 @@
         pltpu.VMEM((ROWS, WIDTH), BF16),
         pltpu.VMEM((8,) + tile, BF16),
         pltpu.VMEM((8,) + tile, BF16),
-        pltpu.VMEM((16, 8, WIDTH), F32),
-        pltpu.VMEM((16, 8, WIDTH), F32),
+        pltpu.VMEM((16, 16, WIDTH // 2), BF16),
+        pltpu.VMEM((16, 16, WIDTH // 2), BF16),
         pltpu.VMEM((2 * ROWS, 2 * ROWS), BF16),
+        pltpu.VMEM((ROWS, 2 * ROWS), F32),
         pltpu.VMEM((padded, 2 * ROWS), F32),
         pltpu.VMEM((ROWS, WIN), F32),
         pltpu.VMEM(tile, F32),
@@ -702,7 +739,7 @@
         uvqk[0], residual[0], lengths, time_buckets, pos_table, time_table,
         output_norm_gain[None], w_out, cotangent[0],
     )
-    steps = 4
+    steps = 2
     some = ROWS // steps
 
     def whole(*shape):

time: 70.4 us -> 64.7 us (0.919)
  Pallas kernels: 69.5 us -> 63.9 us
    pallas_call x1, Pallas kernels: 65.6 us -> 61.1 us  [body(): pl.pallas_call(kernel, out_shape=(jax.ShapeDtypeStruct((ROWS, WIDTH), BF1...]
    pallas_call x1, Pallas kernels: 3.97 us -> 2.82 us  [body(): pl.pallas_call(finish, grid=(steps,), out_shape=(jax.ShapeDtypeStruct((RO...]
where the time goes in v3:
time: 64.7 us; the launch traced here: 64.5 us
  Pallas kernels  63.9 us (99%)
    pallas_call x1, Pallas kernels, body(): pl.pallas_call(kernel, out_shape=(jax.ShapeDtypeStruct((ROWS, WIDTH), BF1...  61.1 us
    pallas_call x1, Pallas kernels, body(): pl.pallas_call(finish, grid=(steps,), out_shape=(jax.ShapeDtypeStruct((RO...  2.82 us

profile of v3, /device:TPU:1, one launch (start us, length us, event | category | flops | bytes accessed | tf_op | source)
XLA Modules:
  0.0 64.5 jit_solution(8441504877503329577)
XLA Ops:
  0.6 61.1 %shard_map.136 = (bf16[128,1024]{1,0:T(8,128)(2,1)}, bf16[128,1024]{1,0:T(8,128)(2,1)}, bf16[8,128,128]{2,1,0:T(8,128)(2,1)}, bf16[8,2,128,128]{3,2,1,0:T(8,128)...) custom-call(bf16[128,4096]{1,0:T(8,128)(2,1)} %bitcast.7, ...), custom_call_target="tpu_custom_call" | custom-call | tf_op jit(solution)/shard_map/pallas_call | solution.py:720
  61.7 2.8 %shard_map.137 = (bf16[128,1024]{1,0:T(8,128)(2,1)}, bf16[128,4096]{1,0:T(8,128)(2,1)}, f32[8,1024]{1,0:T(8,128)}, f32[1,1024]{1,0:T(1,128)}, f32[8,16]{1,0:T(8,128)}, /*index=5*/f32[8,16]{1,0:T(8,128)}) custom-call(bf16[128,4096]{1,0:T(8,128)(2,1)} %bitcast.8, bf16[128,1024]{1,0:T(8,128)(2,1)} %get-tuple-element.20.out_k, ...), custom_call_target="tpu_custom_call" | custom-call | tf_op jit(solution)/shard_map/pallas_call | solution.py:751

commit v4 on v3

--- a/solution.py
+++ b/solution.py
@@ -16,6 +16,7 @@
 SPAN = 9
 WIN = SPAN * ROWS
 PAD = SPAN - 1
+FAR_FIRST = (5, 3, 4, 7, 1, 2, 6)
 WIDTH = HEADS * ROWS
 BUCKETS = 16
 FAR = 131072.0
@@ -170,7 +171,7 @@
         at = 2 * ((y + 4 - k) % 4) + r
         return remote(cot8.at[at], cot8.at[at], cfs.at[k], cfr.at[k], (dp, sib))
 
-    for k in range(1, CHIPS):
+    for k in FAR_FIRST:
         m1(k).start()
     own_fw.start()
 
@@ -240,18 +241,15 @@
             tile = jnp.where(gap < 0, -4096.0, tile)
         pbias[:, pl.ds(w * ROWS, ROWS)] = tile
 
-    for k in range(1, CHIPS):
+    for k in FAR_FIRST:
         m3(k).start()
     own_fv.start()
 
     for k in range(1, CHIPS):
         m1(k).wait_recv()
         fw(k).start()
-    own_fw.wait_recv()
-    for k in range(1, CHIPS):
-        fw(k).wait_recv()
-
-    for k in range(1, CHIPS):
+
+    for k in FAR_FIRST:
         m2(k).start()
 
     ends = [lens[0, 0]]
@@ -272,7 +270,11 @@
         kext[at, pl.ds(0, ROWS)] = rb[block, pl.ds(KEY, ROWS), :]
         return 0
 
-    lax.fori_loop(0, 2 * CHIPS, features, 0)
+    lax.fori_loop(0, CHIPS, lambda k, x: features(2 * k + r, x), 0)
+    own_fw.wait_recv()
+    for k in range(1, CHIPS):
+        fw(k).wait_recv()
+    lax.fori_loop(0, CHIPS, lambda k, x: features(2 * k + 1 - r, x), 0)
 
     def att_copy(k):
         t = (c + k) % CHIPS
@@ -327,6 +329,11 @@
             att_t[t] = jnp.transpose(total)
 
         for_reach(t, run)
+
+        @pl.when(k > 0)
+        def _():
+            att_copy(k).start()
+
         tr = att_t[t]
         mean = jnp.sum(tr, axis=0, keepdims=True) * (1.0 / ROWS)
         dev = tr - mean
@@ -361,10 +368,8 @@
             stats.at[source], stats.at[source], sts.at[k], str_.at[k], (dp, 2 * source + r)
         )
 
-    for k in range(1, CHIPS):
+    for k in FAR_FIRST:
         stat_copy(k).start()
-    for k in range(1, CHIPS):
-        att_copy(k).start()
     att_r[c] = att_s[c]
     for k in range(1, 4):
         cy(k).wait_recv()
@@ -437,7 +442,7 @@
         tmat[...] += dot(hot, high, TN) + dot(hot, low, TN)
         return 0
 
-    lax.fori_loop(0, 2, backward, 0)
+    lax.fori_loop(0, 1, backward, 0)
 
     mine = pl.ds(c, 1)
     mean_c = jnp.transpose(jnp.broadcast_to(comb[0, mine, :], (ROWS, ROWS)))
@@ -472,7 +477,7 @@
         hid_to(j).start()
     hid8[spot] = hid_s[spot]
 
-    lax.fori_loop(2, CHIPS, backward, 0)
+    lax.fori_loop(1, CHIPS, backward, 0)
 
     def to_sibling(t, _):
         at = pl.ds(pl.multiple_of((2 * t + (1 - r) + PAD) * ROWS, ROWS), ROWS)

time: 64.7 us -> 63.5 us (0.981)
  Pallas kernels: 63.9 us -> 62.6 us
    pallas_call x1, Pallas kernels: 61.1 us -> 59.8 us  [body(): pl.pallas_call(kernel, out_shape=(jax.ShapeDtypeStruct((ROWS, WIDTH), BF1...]
where the time goes in v4:
time: 63.5 us; the launch traced here: 63.3 us
  Pallas kernels  62.6 us (99%)
  between operations  0.64 us (1%)
    pallas_call x1, Pallas kernels, body(): pl.pallas_call(kernel, out_shape=(jax.ShapeDtypeStruct((ROWS, WIDTH), BF1...  59.8 us
    pallas_call x1, Pallas kernels, body(): pl.pallas_call(finish, grid=(steps,), out_shape=(jax.ShapeDtypeStruct((RO...  2.82 us

profile of v4, /device:TPU:1, one launch (start us, length us, event | category | flops | bytes accessed | tf_op | source)
XLA Modules:
  0.0 63.3 jit_solution(2646122243381552632)
XLA Ops:
  0.6 59.8 %shard_map.136 = (bf16[128,1024]{1,0:T(8,128)(2,1)}, bf16[128,1024]{1,0:T(8,128)(2,1)}, bf16[8,128,128]{2,1,0:T(8,128)(2,1)}, bf16[8,2,128,128]{3,2,1,0:T(8,128)...) custom-call(bf16[128,4096]{1,0:T(8,128)(2,1)} %bitcast.7, ...), custom_call_target="tpu_custom_call" | custom-call | tf_op jit(solution)/shard_map/pallas_call | solution.py:725
  60.5 2.8 %shard_map.137 = (bf16[128,1024]{1,0:T(8,128)(2,1)}, bf16[128,4096]{1,0:T(8,128)(2,1)}, f32[8,1024]{1,0:T(8,128)}, f32[1,1024]{1,0:T(1,128)}, f32[8,16]{1,0:T(8,128)}, /*index=5*/f32[8,16]{1,0:T(8,128)}) custom-call(bf16[128,4096]{1,0:T(8,128)(2,1)} %bitcast.8, bf16[128,1024]{1,0:T(8,128)(2,1)} %get-tuple-element.20.out_k, ...), custom_call_target="tpu_custom_call" | custom-call | tf_op jit(solution)/shard_map/pallas_call | solution.py:756

commit v5 on v4

--- a/solution.py
+++ b/solution.py
@@ -56,8 +56,8 @@
 
 def kernel(
     uvqk_h, resid_h, lens, times, ptab, ttab, gain, wout_h, cot_h,
-    out, dpu, mq_r, mk_r, dwo, dgain, dpos, dtime,
-    uvqk, resid, wout, cot8, sb, rb, dh, kext, vall, wa, pbias, wsave, fsave,
+    out_h, dpu_h, mq_r, mk_r, dwo, dgain, dpos, dtime,
+    out, dpu, uvqk, resid, wout, cot8, sb, rb, dh, kext, vall, wa, pbias, wsave, fsave,
     att_t, pn_t, gcol, att_s, att_r, stats, comb, dout, hid, hid_s, hid8,
     e_s, e_r, diag, dq_t, dkv, pacc, tmat, gacc, mq_s, xs, xr, mk_s, tab1, tab2,
     loc_sem, m1s, m1r, m2s, m2r, m3s, m3r, fws, fwr, fvs, fvr, sib_s, sib_r, ats, atr, sts, str_,
@@ -464,6 +464,8 @@
         return 0
 
     lax.fori_loop(0, HEADS, rows_of, 0)
+    store_dpu = pltpu.make_async_copy(dpu, dpu_h, loc_sem.at[7])
+    store_dpu.start()
 
     def hid_to(j):
         y_to = (y + j // 2) % 4
@@ -594,10 +596,14 @@
         return 0
 
     lax.fori_loop(0, CHIPS, join, 0)
-    mq_r[c] = mq_s[c]
-    mk_r[c] = mk_s[c]
+    own_dq = pltpu.make_async_copy(mq_s.at[c], mq_r.at[c], loc_sem.at[4])
+    own_kv = pltpu.make_async_copy(mk_s.at[c], mk_r.at[c], loc_sem.at[5])
+    own_dq.start()
+    own_kv.start()
     load_resid.wait()
     out[...] = (resid[...].astype(F32) + dot(hid[...], wout[...])).astype(BF16)
+    store_out = pltpu.make_async_copy(out, out_h, loc_sem.at[6])
+    store_out.start()
 
 
     for k in range(1, 16):
@@ -627,6 +633,10 @@
     for k in range(1, CHIPS):
         kv_copy(k).wait_recv()
 
+    own_dq.wait()
+    own_kv.wait()
+    store_out.wait()
+    store_dpu.wait()
     own_fw.wait_send()
     own_fv.wait_send()
     dkv_copy.wait_send()
@@ -676,6 +686,8 @@
     dma = pltpu.SemaphoreType.DMA
     padded = (2 * CHIPS + PAD) * ROWS
     scratch = [
+        pltpu.VMEM((ROWS, WIDTH), BF16),
+        pltpu.VMEM((ROWS, WIDTH), BF16),
         pltpu.VMEM((ROWS, 4 * WIDTH), BF16),
         pltpu.VMEM((ROWS, WIDTH), BF16),
         pltpu.VMEM((WIDTH, WIDTH), BF16),
@@ -714,7 +726,7 @@
         pltpu.VMEM((CHIPS, 2) + tile, BF16),
         pltpu.VMEM((8, 8, ROWS), F32),
         pltpu.VMEM((16, 8, ROWS), F32),
-        dma((4,)),
+        dma((8,)),
     ] + [
         dma((count,))
         for count in (
@@ -735,7 +747,7 @@
             jax.ShapeDtypeStruct((HEADS, BUCKETS), F32),
         ),
         in_specs=[hbm, hbm, sm, vm, sm, sm, vm, hbm, hbm],
-        out_specs=(vm,) * 8,
+        out_specs=(hbm,) * 4 + (vm,) * 4,
         scratch_shapes=scratch,
         compiler_params=pltpu.CompilerParams(
             collective_id=0, has_side_effects=True, vmem_limit_bytes=63 * 1024 * 1024

time: 63.5 us -> 63.1 us (level)
  no operation moved by 1% of the time
where the time goes in v5:
time: 63.1 us; the launch traced here: 62.9 us
  Pallas kernels  62.3 us (99%)
  between operations  0.64 us (1%)
    pallas_call x1, Pallas kernels, body(): pl.pallas_call(kernel, out_shape=(jax.ShapeDtypeStruct((ROWS, WIDTH), BF1...  59.5 us
    pallas_call x1, Pallas kernels, body(): pl.pallas_call(finish, grid=(steps,), out_shape=(jax.ShapeDtypeStruct((RO...  2.82 us

profile of v5, /device:TPU:1, one launch (start us, length us, event | category | flops | bytes accessed | tf_op | source)
XLA Modules:
  0.0 62.9 jit_solution(3023638624144405952)
XLA Ops:
  0.6 59.5 %shard_map.136 = (bf16[128,1024]{1,0:T(8,128)(2,1)}, bf16[128,1024]{1,0:T(8,128)(2,1)}, bf16[8,128,128]{2,1,0:T(8,128)(2,1)}, bf16[8,2,128,128]{3,2,1,0:T(8,128)...) custom-call(bf16[128,4096]{1,0:T(8,128)(2,1)} %bitcast.7, ...), custom_call_target="tpu_custom_call" | custom-call | tf_op jit(solution)/shard_map/pallas_call | solution.py:737
  60.1 2.8 %shard_map.137 = (bf16[128,1024]{1,0:T(8,128)(2,1)}, bf16[128,4096]{1,0:T(8,128)(2,1)}, f32[8,1024]{1,0:T(8,128)}, f32[1,1024]{1,0:T(1,128)}, f32[8,16]{1,0:T(8,128)}, /*index=5*/f32[8,16]{1,0:T(8,128)}) custom-call(bf16[128,4096]{1,0:T(8,128)(2,1)} %bitcast.8, bf16[128,1024]{1,0:T(8,128)(2,1)} %get-tuple-element.20.out_k, ...), custom_call_target="tpu_custom_call" | custom-call | tf_op jit(solution)/shard_map/pallas_call | solution.py:768
